TPU v7x, 512 devices: a whole 4x8x8 slice. The times are simulated.
512 devices in a mesh: dp: 64 (over z, y), tensor: 8 (over x, core).
Axes of the slice: x: 4, y: 8, z: 8, core: 2. Of those that a mesh axis runs over, the one named last changes fastest.
Arguments:
- activations: bfloat16 [16384, 4096], P(('dp', 'tensor')), may hold values from -24 to 24
- cotangent: bfloat16 [16384, 4096], P(('dp', 'tensor')), may hold values from -24 to 24
- gate_pre: bfloat16 [16384, 16384], P('dp', 'tensor'), may hold values from -8 to 8
- up_value: bfloat16 [16384, 16384], P('dp', 'tensor'), may hold values from -6 to 6
- hidden_grad: bfloat16 [16384, 16384], P('dp', 'tensor'), may hold values from -16 to 16
- warm_factors: float32 [2, 8, 4096, 128], P(None, 'tensor', 'dp'), may hold values from -6 to 6
Outputs:
- left_united: float32 [8, 4096, 128], P('tensor', 'dp')
- left_down: float32 [8, 2048, 128], P('tensor', 'dp')
- right_factors: float32 [2, 8, 4096, 128], P(None, 'tensor', 'dp')
All inputs are finite; a program needn't handle non-finite values.
Results may differ from a plain program's by a relative error of at most 0.0031.
Values may be sent and summed in bfloat16 or wider, within the bound.
A program may use at most 64 MiB of HBM per device.

v0:
```python
import jax
import jax.numpy as jnp
from jax import lax
from jax.sharding import PartitionSpec as P


def cholesky_columns(matrix):
    gram_matrix = jnp.dot(matrix.T, matrix, precision=lax.Precision.HIGHEST)
    lower_factor = jnp.linalg.cholesky(gram_matrix)
    solved = lax.linalg.triangular_solve(lower_factor, matrix.T, left_side=True, lower=True)
    return solved.T


def make_orthonormal(matrix):
    return cholesky_columns(matrix)


def on_device(activations, cotangent, gate_pre, up_value, hidden_grad, warm_factors):
    acts_all, cotan_all = (
        lax.all_gather(activations, "tensor", axis=0, tiled=True),
        lax.all_gather(cotangent, "tensor", axis=0, tiled=True),
    )
    gate_wide = gate_pre.astype(jnp.float32)
    up_wide = up_value.astype(jnp.float32)
    hgrad_wide = hidden_grad.astype(jnp.float32)
    sigma = jax.nn.sigmoid(gate_wide)
    active = gate_wide * sigma
    hidden = (active * up_wide).astype(jnp.bfloat16)
    gate_back = (hgrad_wide * up_wide * sigma * (1.0 + gate_wide * (1.0 - sigma))).astype(
        jnp.bfloat16
    )
    up_back = (hgrad_wide * active).astype(jnp.bfloat16)
    united_back = jnp.concatenate([gate_back, up_back], axis=1)
    piece = lax.all_gather(warm_factors, "dp", axis=2, tiled=True)
    first = jnp.einsum(
        "td,dr->tr",
        acts_all,
        piece[0, 0],
        precision=lax.Precision.HIGHEST,
        preferred_element_type=jnp.float32,
    )
    second = jnp.einsum(
        "td,dr->tr",
        cotan_all,
        piece[1, 0],
        precision=lax.Precision.HIGHEST,
        preferred_element_type=jnp.float32,
    )
    raw_united = jnp.einsum(
        "tf,tr->fr",
        united_back,
        first,
        precision=lax.Precision.HIGHEST,
        preferred_element_type=jnp.float32,
    )
    raw_down = jnp.einsum(
        "tf,tr->fr",
        hidden,
        second,
        precision=lax.Precision.HIGHEST,
        preferred_element_type=jnp.float32,
    )
    replicas = lax.axis_size("dp")
    place = lax.axis_index("dp")

    def right_term(columns_source, mixed):
        return (
            jnp.einsum(
                "td,tr->dr",
                columns_source,
                mixed,
                precision=lax.Precision.HIGHEST,
                preferred_element_type=jnp.float32,
            )
            / replicas
        )

    left_one = make_orthonormal(lax.psum(raw_united, "dp"))
    mixed_one = jnp.einsum(
        "tf,fr->tr",
        united_back,
        left_one,
        precision=lax.Precision.HIGHEST,
        preferred_element_type=jnp.float32,
    )
    right_one = lax.psum_scatter(
        right_term(acts_all, mixed_one), "dp", scatter_dimension=0, tiled=True
    )
    left_two = make_orthonormal(lax.psum(raw_down, "dp"))
    mixed_two = jnp.einsum(
        "tf,fr->tr",
        hidden,
        left_two,
        precision=lax.Precision.HIGHEST,
        preferred_element_type=jnp.float32,
    )
    right_two = lax.psum_scatter(
        right_term(cotan_all, mixed_two), "dp", scatter_dimension=0, tiled=True
    )
    share_united = left_one.shape[0] // replicas
    share_down = left_two.shape[0] // replicas
    mine_united = lax.dynamic_slice_in_dim(left_one, place * share_united, share_united, 0)
    mine_down = lax.dynamic_slice_in_dim(left_two, place * share_down, share_down, 0)
    right_stack = jnp.stack([right_one, right_two])
    return (mine_united[None], mine_down[None], right_stack[:, None])


def solution(mesh):
    in_specs = (
        P(("dp", "tensor"), None),
        P(("dp", "tensor"), None),
        P("dp", "tensor"),
        P("dp", "tensor"),
        P("dp", "tensor"),
        P(None, "tensor", "dp", None),
    )
    out_specs = (P("tensor", "dp", None), P("tensor", "dp", None), P(None, "tensor", "dp", None))
    return jax.shard_map(
        on_device, mesh=mesh, in_specs=in_specs, out_specs=out_specs, check_vma=False
    )
```

profile of v0, /device:TPU:6, one launch (start us, length us, event | category | flops | bytes accessed | tf_op | source)
XLA Modules:
  0.0 868.3 jit_solution(4832438889304783815)
XLA Ops:
  9.4 3.3 fusion.6
  12.7 31.6 %all-gather.8.cloned.1.call-done = bf16[256,4096]{1,0:T(8,128)(2,1)} async-done(((bf16[32,4096]{1,0:T(8,128)(2,1)}), bf16[256,4096]{1,0:T(8,128)(2,1)}) %all-gather.8.cloned.1.call-update) | async-done | bytes 2097168 | tf_op jit(solution)/shard_map/all_gather | solution.py:21
  44.3 91.5 %all-gather.6.cloned.1.call-done = f32[2,1,4096,128]{3,2,1,0:T(8,128)} async-done(((f32[2,1,64,128]{3,2,1,0:T(8,128)}), f32[2,1,4096,128]{3,2,1,0:T(8,128)}) %all-gather.6.cloned.1.call-update) | async-done | bytes 4194320 | tf_op jit(solution)/shard_map/all_gather | solution.py:34
  135.8 4.1 fusion.11
  139.9 2.2 fusion.26
  142.0 22.2 %all-gather.4.cloned.1.call-done = bf16[256,4096]{1,0:T(8,128)(2,1)} async-done(((bf16[32,4096]{1,0:T(8,128)(2,1)}), bf16[256,4096]{1,0:T(8,128)(2,1)}) %all-gather.4.cloned.1.call-update) | async-done | bytes 2097168 | tf_op jit(solution)/shard_map/all_gather | solution.py:20
  164.2 4.1 fusion.12
  168.3 3.6 fusion.14
  172.2 168.4 %all-reduce.3.cloned.1.call-done = (f32[4096,128]{1,0:T(8,128)}, f32[2048,128]{1,0:T(8,128)}) async-done(((f32[4096,128]{1,0:T(8,128)}, f32[2048,128]{1,0:T(8,128)}), (f32[4096,128]{1,0:T(8,128)}, f32[2048,128]{1,0:T(8,128)})) %all-reduce.3.cloned.1.call-update) | async-done | bytes 3145744 | tf_op jit(solution)/shard_map/psum | solution.py:78
  340.6 3.4 fusion.27
  344.2 11.7 %cholesky.55 = f32[128,128]{1,0:T(8,128)S(1)} custom-call(f32[128,128]{1,0:T(8,128)S(1)} %fusion.19), custom_call_target="Cholesky" | custom-call | tf_op jit(solution)/shard_map/jit(cholesky)/cholesky | solution.py:9
  357.2 9.8 %custom-call.9 = f32[1,128,128]{1,2,0:T(8,128)S(1)} custom-call(f32[1,128,128]{2,1,0:T(8,128)S(1)} %fusion.16), custom_call_target="InvertDiagBlocksLowerTriangular" | custom-call | tf_op jit(solution)/shard_map/triangular_solve | solution.py:10
  367.1 1.1 fusion.17
  368.1 1.0 fusion.28
  369.2 1.0 fusion
  370.2 1.9 copy.21
  372.4 1.3 copy-done
  373.7 3.5 fusion.25
  377.2 11.7 %cholesky.44 = f32[128,128]{1,0:T(8,128)S(1)} custom-call(f32[128,128]{1,0:T(8,128)S(1)} %fusion.22), custom_call_target="Cholesky" | custom-call | tf_op jit(solution)/shard_map/jit(cholesky)/cholesky | solution.py:9
  390.3 9.8 %custom-call.8 = f32[1,128,128]{1,2,0:T(8,128)S(1)} custom-call(f32[1,128,128]{2,1,0:T(8,128)S(1)} %fusion.15), custom_call_target="InvertDiagBlocksLowerTriangular" | custom-call | tf_op jit(solution)/shard_map/triangular_solve | solution.py:10
  400.1 2.0 fusion.20
  402.1 2.1 fusion.13
  404.5 1.0 fusion.1
  405.5 1.8 copy.19
  407.4 0.9 dynamic-slice_bitcast_fusion
  409.0 0.9 dynamic-slice_bitcast_fusion.1
  409.9 0.7 copy.16
  410.6 203.0 %reduce-scatter.9.cloned.1.call-done = f32[64,128]{1,0:T(8,128)} async-done(((f32[4096,128]{1,0:T(8,128)}), f32[64,128]{1,0:T(8,128)}) %reduce-scatter.9.cloned.1.call-update) | async-done | bytes 32784
  613.6 0.8 copy.22
  614.5 245.4 %reduce-scatter.7.cloned.1.call-done = f32[64,128]{1,0:T(8,128)} async-done(((f32[4096,128]{1,0:T(8,128)}), f32[64,128]{1,0:T(8,128)}) %reduce-scatter.7.cloned.1.call-update) | async-done | bytes 32784
  859.9 0.8 copy.20
  860.8 0.7 copy.18
  (39 shorter events, 6.5 us)
Async XLA Ops:
  7.2 37.2 %all-gather.8.cloned.1.call-start = ((), (), s32[]{:S(2)}) async-start(), calls=%async_computation.4 | async-start | bytes 2359296 | tf_op jit(solution)/shard_map/all_gather | solution.py:21
  7.9 127.9 %all-gather.6.cloned.1.call-start = ((), (), s32[]{:S(2)}) async-start(), calls=%async_computation.3 | async-start | bytes 4259840 | tf_op jit(solution)/shard_map/all_gather | solution.py:34
  8.6 155.6 %all-gather.4.cloned.1.call-start = ((), (), s32[]{:S(2)}) async-start(), calls=%async_computation.2 | async-start | bytes 2359296 | tf_op jit(solution)/shard_map/all_gather | solution.py:20
  9.4 331.2 %all-reduce.3.cloned.1.call-start = ((), (), s32[]{:S(2)}) async-start(), calls=%async_computation.7 | async-start | bytes 6291456 | tf_op jit(solution)/shard_map/psum | solution.py:78
  12.7 155.6 %copy-start.2 = (bf16[256,2048]{1,0:T(8,128)(2,1)}, bf16[256,2048]{1,0:T(8,128)(2,1)S(1)}, u32[]{:S(2)}) copy-start(bf16[256,2048]{1,0:T(8,128)(2,1)S(1)} %get-tuple-element.14) | copy-start | bytes 3145732
  172.0 441.6 %reduce-scatter.9.cloned.1.call-start = ((), (), s32[]{:S(2)}) async-start(), calls=%async_computation.6 | async-start | bytes 2129920
  340.6 26.4 %copy-start.1 = (f32[2048,128]{1,0:T(8,128)S(1)}, f32[2048,128]{1,0:T(8,128)}, u32[]{:S(2)}) copy-start(f32[2048,128]{1,0:T(8,128)} %get-tuple-element.11) | copy-start | bytes 3145732
  367.0 2.1 copy-start.6
  368.1 1.0 copy-start.7
  372.1 1.6 copy-start
  372.1 487.8 %reduce-scatter.7.cloned.1.call-start = ((), (), s32[]{:S(2)}) async-start(), calls=%async_computation.5 | async-start | bytes 2129920
  400.1 2.0 copy-start.3
  402.1 2.2 copy-start.4
  402.1 2.4 copy-start.5
Sparse Core Ops, SparseCore 0:
  10.2 34.1 all-gather.7
  47.3 88.4 all-gather.5
  137.9 26.2 all-gather.3
  172.1 168.4 all-reduce.2
  372.2 241.3 reduce-scatter.8
  618.1 241.7 reduce-scatter.6
where the time goes:
time: 869 us; the launch traced here: 868 us
  waiting for transfers between devices  764 us (88%)
  other arithmetic  49 us (6%)
  matrix products  29 us (3%)
  between operations  14.4 us (2%)
  local copies, waits for them, and re-layouts  11 us (1%)
    unnamed x8, waiting for transfers between devices  451 us
    psum x1, waiting for transfers between devices, on_device(): left_one = make_orthonormal(lax.psum(raw_united, 'dp'))  168 us
    all_gather x1, waiting for transfers between devices, on_device(): piece = lax.all_gather(warm_factors, 'dp', axis=2, tiled=True)  91.5 us
    all_gather x1, waiting for transfers between devices, on_device(): lax.all_gather(cotangent, 'tensor', axis=0, tiled=True)  31.6 us
    another operation x6, other arithmetic, cholesky_columns(): lower_factor = jnp.linalg.cholesky(gram_matrix)  24.8 us
    all_gather x1, waiting for transfers between devices, on_device(): lax.all_gather(activations, 'tensor', axis=0, tiled=True)  22.2 us
    another operation x4, other arithmetic, cholesky_columns(): lax.linalg.triangular_solve(lower_factor, matrix.T, left_side=True, lower...  20.9 us
  transfers between devices with their start and end apart: 6, of which 6 were waited for; matrix products, arithmetic and copies ran while one was open for 5% of the time, Pallas kernels for 0%

commit v1 on v0

v1 whole, which is shorter than its diff:
```python
import functools

import jax
import jax.numpy as jnp
from jax import lax
from jax.experimental import pallas as pl
from jax.experimental.pallas import tpu as pltpu
from jax.sharding import PartitionSpec as P

F32 = jnp.float32
BF16 = jnp.bfloat16
RANK = 128
CUT = 48
PANEL = 16


def tdot(left, right):
    return lax.dot_general(left, right, (((0,), (0,)), ((), ())), preferred_element_type=F32)


def two_halves(values):
    high = values.astype(BF16)
    low = (values - high.astype(F32)).astype(BF16)
    return jnp.concatenate([high, low], axis=1)


def kernel(nz, ny, nt, acts_in, cot_in, gate_in, up_in, hg_in, warm_in,
           left_u_out, left_d_out, right_out,
           acts, cot, gate, up, hg, warm,
           gate_back, up_back, hidden,
           part_a, part_b, got_a, got_b, sum_a, sum_b, fin_a, fin_b,
           raw_u, raw_d, all_u, all_d,
           rpart_a, rpart_b, rgot_a, rgot_b, rsum_a, rsum_b, rfin_a, rfin_b,
           gram,
           load_sem, tok_send, tok_recv, first_send, first_recv,
           ring_send, ring_recv, one_send, one_recv, two_send, two_recv):
    d = lax.axis_index("dp")
    t = lax.axis_index("tensor")
    z, y = d // ny, d % ny
    nx = nt // 2
    x, c = t // 2, t % 2
    tokens = acts_in.shape[0]
    width = acts_in.shape[1]
    ff = gate_in.shape[1]
    tile = ny * 64

    def at_z(p):
        return {"dp": p * ny + y}

    def at_y(p):
        return {"dp": z * ny + p}

    def slot(xx, cc):
        return (xx % nx) * 2 + cc

    def remote(src, dst, send, recv, where):
        return pltpu.make_async_remote_copy(
            src_ref=src, dst_ref=dst, send_sem=send, recv_sem=recv,
            device_id=where, device_id_type=pl.DeviceIdType.MESH)

    loads = [
        pltpu.make_async_copy(src, dst, load_sem.at[i])
        for i, (src, dst) in enumerate([
            (warm_in.at[0, 0], warm.at[0, z, y]), (warm_in.at[1, 0], warm.at[1, z, y]),
            (gate_in, gate), (up_in, up), (hg_in, hg),
            (acts_in, acts.at[t]), (cot_in, cot.at[t])])
    ]
    for load in loads:
        load.start()

    barrier = pltpu.get_barrier_semaphore()
    to_right = {"tensor": slot(x + 1, c)}
    to_left = {"tensor": slot(x + nx - 1, c)}
    to_twin = {"tensor": slot(x, 1 - c)}

    def greet(where):
        pl.semaphore_signal(barrier, inc=1, device_id=where, device_id_type=pl.DeviceIdType.MESH)

    for where in (to_right, to_left, to_twin):
        greet(where)
    for k in range(1, nz):
        greet(at_z((z + k) % nz))
    for k in range(1, ny):
        greet(at_y((y + k) % ny))
    for load in loads[:2]:
        load.wait()
    pl.semaphore_wait(barrier, 3 + nz - 1 + ny - 1)

    def exchange(n, me, place, src, dst, send, recv):
        for k in range(1, n):
            to = (me + k) % n
            remote(src(to), dst(k, me), send.at[k - 1], recv.at[k - 1], place(to)).start()

    def landed(n, me, place, src, dst, send, recv, k):
        owner = (me + n - k) % n
        return remote(src(owner), dst(k, owner), send.at[k - 1], recv.at[k - 1], place(owner))

    def first_phase(which, pieces):
        plans = []
        for i, (along_y, block) in enumerate(pieces):
            if along_y:
                plan = (ny, y, at_y, lambda to, b=block: b(z, y), lambda k, o, b=block: b(z, o))
            else:
                plan = (nz, z, at_z, lambda to, b=block: b(z, y), lambda k, o, b=block: b(o, y))
            plans.append(plan + (first_send.at[which, i], first_recv.at[which, i]))
        return plans

    def start_first(plans):
        for plan in plans:
            exchange(*plan)

    def wait_first(plans):
        for plan in plans:
            for k in range(1, plan[0]):
                landed(*plan, k).wait_recv()

    def drain_first(plans):
        for plan in plans:
            for k in range(1, plan[0]):
                landed(*plan, k).wait_send()

    def ring_copies(streams, step, half, i, receiving):
        n, me, place, pieces, turn, which = streams[i]
        if receiving:
            block = (me + n - turn * (1 + step)) % n
        else:
            block = (me + n - turn * step) % n
        to = (me + n + turn) % n
        return [
            remote(ref, ref, ring_send.at[which, i, step, half, j],
                   ring_recv.at[which, i, step, half, j], place(to))
            for j, ref in enumerate(pieces(block, half))
        ]

    def ring_moves(n, turn, step):
        if step < n // 2 - 1:
            return (0, 1) if turn > 0 else (1, 0)
        return (0,) if turn > 0 else (1,)

    def ring_start(streams):
        for order in range(2):
            for i, (n, _, _, _, turn, _) in enumerate(streams):
                halves = ring_moves(n, turn, 0)
                if order < len(halves):
                    for copy in ring_copies(streams, 0, halves[order], i, False):
                        copy.start()

    def ring_advance(streams, step):
        for order in range(2):
            for i, (n, _, _, _, turn, _) in enumerate(streams):
                if step >= n // 2:
                    continue
                halves = ring_moves(n, turn, step)
                if order < len(halves):
                    half = halves[order]
                    for copy in ring_copies(streams, step, half, i, True):
                        copy.wait_recv()
                    if step + 1 < n // 2 and half in ring_moves(n, turn, step + 1):
                        for copy in ring_copies(streams, step + 1, half, i, False):
                            copy.start()

    def ring_drain(streams):
        for i, (n, _, _, _, turn, _) in enumerate(streams):
            for step in range(n // 2):
                for half in ring_moves(n, turn, step):
                    for copy in ring_copies(streams, step, half, i, False):
                        copy.wait_send()

    def ring_streams(which, z_pieces, y_pieces):
        return [
            (nz, z, at_z, z_pieces, 1, which), (nz, z, at_z, z_pieces, -1, which),
            (ny, y, at_y, y_pieces, 1, which), (ny, y, at_y, y_pieces, -1, which)]

    here = slot(x, c)
    behind, ahead, across = slot(x + nx - 1, c), slot(x + 1, c), slot(x + 2, c)
    twin = [slot(x, 1 - c), slot(x + nx - 1, 1 - c), slot(x + 1, 1 - c), slot(x + 2, 1 - c)]
    tok_sends = []

    def tok(i, src, dst, where):
        copy = remote(src, dst, tok_send.at[i], tok_recv.at[i], where)
        copy.start()
        tok_sends.append(copy)

    def tok_wait(i, ref):
        remote(ref, ref, tok_send.at[i], tok_recv.at[i], to_twin).wait_recv()

    warm_first = first_phase(0, [
        (True, lambda zz, yy: warm.at[0, zz, yy]), (False, lambda zz, yy: warm.at[1, zz, yy])])
    start_first(warm_first)
    tok(0, acts_in, acts.at[here], to_right)
    tok(3, cot_in, cot.at[here], to_left)
    tok(1, cot_in, cot.at[here], to_right)
    tok(2, acts_in, acts.at[here], to_left)
    tok(6, acts_in, acts.at[here], to_twin)
    tok(10, cot_in, cot.at[here], to_twin)

    for load in loads[2:5]:
        load.wait()

    def backward(i, carry):
        rows = pl.ds(pl.multiple_of(i * 16, 16), 16)
        gate_w = gate[rows, :].astype(F32)
        up_w = up[rows, :].astype(F32)
        hg_w = hg[rows, :].astype(F32)
        sigma = jax.nn.sigmoid(gate_w)
        active = gate_w * sigma
        hidden[rows, :] = (active * up_w).astype(BF16)
        gate_back[rows, :] = (hg_w * up_w * sigma * (1.0 + gate_w * (1.0 - sigma))).astype(BF16)
        up_back[rows, :] = (hg_w * active).astype(BF16)
        return carry

    steps = gate_in.shape[0] // 16
    lax.fori_loop(0, steps // 2, backward, 0)

    wait_first(warm_first)
    halves_y, halves_z = ny // 2, nz // 2
    warm_ring = ring_streams(
        0,
        lambda b, h: [warm.at[0, b, pl.ds(h * halves_y, halves_y)]],
        lambda b, h: [warm.at[1, pl.ds(h * halves_z, halves_z), b]])
    ring_start(warm_ring)
    lax.fori_loop(steps // 2, steps, backward, 0)

    tok_wait(0, acts.at[behind])
    tok(4, acts.at[behind], acts.at[behind], to_right)
    tok(7, acts.at[behind], acts.at[behind], to_twin)
    tok_wait(3, cot.at[ahead])
    tok(5, cot.at[ahead], cot.at[ahead], to_left)
    tok(12, cot.at[ahead], cot.at[ahead], to_twin)
    ring_advance(warm_ring, 0)
    tok_wait(2, acts.at[ahead])
    tok(8, acts.at[ahead], acts.at[ahead], to_twin)
    tok_wait(1, cot.at[behind])
    tok(11, cot.at[behind], cot.at[behind], to_twin)
    for step in range(1, max(nz, ny) // 2):
        ring_advance(warm_ring, step)
    tok_wait(4, acts.at[across])
    tok(9, acts.at[across], acts.at[across], to_twin)
    tok_wait(5, cot.at[across])
    tok(13, cot.at[across], cot.at[across], to_twin)
    for load in loads[5:]:
        load.wait()
    for i in range(4):
        tok_wait(6 + i, acts.at[twin[i]])
        tok_wait(10 + i, cot.at[twin[i]])

    def probe(tokens_ref, w):
        def body(i, total):
            columns = pl.ds(pl.multiple_of(i * tile, tile), tile)
            rows = tokens_ref[:, :, columns].reshape(nt * tokens, tile)
            factor = two_halves(warm[w, i].reshape(tile, RANK))
            return total + jnp.dot(rows, factor, preferred_element_type=F32)

        pair = lax.fori_loop(0, nz, body, jnp.zeros((nt * tokens, 2 * RANK), F32))
        return two_halves(pair[:, :RANK] + pair[:, RANK:])

    probe_u = probe(acts, 0)
    probe_d = probe(cot, 1)

    def folded(pair):
        return (pair[:, :RANK] + pair[:, RANK:]).astype(BF16)

    per_tile = ff // tile

    def raw_tile(source, first):
        def body(i, carry):
            columns = pl.ds(pl.multiple_of(i * tile, tile), tile)
            block = folded(tdot(source[:, columns], probe_u)).reshape(ny, 64, RANK)
            part_a[first + i] = block[:, :CUT]
            part_b[first + i, :, :64 - CUT] = block[:, CUT:]
            return carry
        return body

    lax.fori_loop(0, per_tile, raw_tile(gate_back, 0), 0)
    lax.fori_loop(0, per_tile, raw_tile(up_back, per_tile), 0)

    sends = []

    def start_one(i, a, b, ga, gb):
        plans = [
            (nz, z, at_z, lambda to: a.at[to], lambda k, o: ga.at[k - 1], one_send.at[i, 0], one_recv.at[i, 0]),
            (ny, y, at_y, lambda to: b.at[:, to], lambda k, o: gb.at[k - 1], one_send.at[i, 1], one_recv.at[i, 1])]
        return plans

    raw_one = start_one(0, part_a, part_b, got_a, got_b)
    exchange(*raw_one[0])

    def down_tile(i, carry):
        columns = pl.ds(pl.multiple_of(i * tile, tile), tile)
        block = folded(tdot(hidden[:, columns], probe_d)).reshape(2, ny, 32, RANK)
        part_b[pl.ds(2 * i, 2), :, 64 - CUT:] = block
        return carry

    lax.fori_loop(0, per_tile, down_tile, 0)
    exchange(*raw_one[1])

    def scatter_rest(i, plans, a, b, ga, gb, sa, sb, fa, fb, done):
        sa[...] = a[z].astype(F32)
        sb[...] = b[:, y].astype(F32)
        two = [
            (ny, y, at_y, lambda to: sa.at[to], lambda k, o: fa.at[k - 1], two_send.at[i, 0], two_recv.at[i, 0]),
            (nz, z, at_z, lambda to: sb.at[to], lambda k, o: fb.at[k - 1], two_send.at[i, 1], two_recv.at[i, 1])]
        for plan, total, got, second in ((plans[0], sa, ga, two[0]), (plans[1], sb, gb, two[1])):
            for k in range(1, plan[0]):
                landed(*plan, k).wait_recv()
                total[...] += got[k - 1].astype(F32)
            exchange(*second)
        for route, (plan, total, fin, me) in enumerate(((two[0], sa, fa, y), (two[1], sb, fb, z))):
            value = total[me]
            for k in range(1, plan[0]):
                landed(*plan, k).wait_recv()
                value = value + fin[k - 1]
            done(route, value)
        return plans + two

    def raw_done(route, value):
        if route == 0:
            raw_u[:CUT] = value
        else:
            raw_u[CUT:] = value[:64 - CUT]
            raw_d[...] = value[64 - CUT:]

    sent = scatter_rest(0, raw_one, part_a, part_b, got_a, got_b, sum_a, sum_b, fin_a, fin_b, raw_done)

    all_u[z, y] = raw_u[...].astype(BF16)
    all_d[z, y] = raw_d[...].astype(BF16)
    raw_first = first_phase(1, [
        (True, lambda zz, yy: all_u.at[zz, yy, pl.ds(0, CUT)]),
        (False, lambda zz, yy: all_u.at[zz, yy, pl.ds(CUT, 64 - CUT)]),
        (False, lambda zz, yy: all_d.at[zz, yy])])
    start_first(raw_first)
    raw_ring = ring_streams(
        1,
        lambda b, h: [all_u.at[b, pl.ds(h * halves_y, halves_y), pl.ds(0, CUT)]],
        lambda b, h: [
            all_u.at[pl.ds(h * halves_z, halves_z), b, pl.ds(CUT, 64 - CUT)],
            all_d.at[pl.ds(h * halves_z, halves_z), b]])
    wait_first(raw_first)
    ring_start(raw_ring)
    for step in range(max(nz, ny) // 2):
        ring_advance(raw_ring, step)

    flat_u = all_u[...].reshape(2 * ff, RANK)
    mixed_u = two_halves(
        jnp.dot(gate_back[...], flat_u[:ff], preferred_element_type=F32)
        + jnp.dot(up_back[...], flat_u[ff:], preferred_element_type=F32))
    flat_d = all_d[...].reshape(ff, RANK)
    mixed_d = two_halves(jnp.dot(hidden[...], flat_d, preferred_element_type=F32))

    def right_tile(source, mixed, target):
        def body(i, carry):
            columns = pl.ds(pl.multiple_of(i * tile, tile), tile)
            rows = source[:, :, columns].reshape(nt * tokens, tile)
            target[i] = folded(tdot(rows, mixed)).reshape(ny, 64, RANK)
            return carry
        return body

    right_one = start_one(1, rpart_a, rpart_b, rgot_a, rgot_b)
    lax.fori_loop(0, nz, right_tile(acts, mixed_u, rpart_a), 0)
    exchange(*right_one[0])
    lax.fori_loop(0, nz, right_tile(cot, mixed_d, rpart_b), 0)
    exchange(*right_one[1])

    row = lax.broadcasted_iota(jnp.int32, (RANK, RANK), 0)
    col = lax.broadcasted_iota(jnp.int32, (RANK, RANK), 1)
    for i, flat in enumerate((flat_u, flat_d)):
        gram[i, :, :RANK] = tdot(flat, flat)
        gram[i, :, RANK:] = (row == col).astype(F32)
    lane = lax.broadcasted_iota(jnp.int32, (PANEL, RANK), 1)
    sub = lax.broadcasted_iota(jnp.int32, (PANEL, RANK), 0)
    sub_one = lax.broadcasted_iota(jnp.int32, (PANEL, 1), 0)

    def eliminate(b, carry):
        base = pl.multiple_of(b * PANEL, PANEL)
        rows = pl.ds(base, PANEL)
        panels = [gram[i, rows, :] for i in range(2)]
        for j in range(PANEL):
            for i in range(2):
                panel = panels[i]
                column = jnp.sum(
                    jnp.where(lane == base + j, panel[:, :RANK], 0.0), axis=1, keepdims=True)
                factor = jnp.where(sub_one > j, column / column[j:j + 1], 0.0)
                panels[i] = panel - factor * panel[j:j + 1]
        for i in range(2):
            panel = panels[i]
            gram[i, rows, :] = panel
            head = panel[:, :RANK]
            pivots = jnp.sum(jnp.where(lane == base + sub, head, 0.0), axis=1, keepdims=True)
            weights = jnp.where(lane >= base + PANEL, head / pivots, 0.0)
            gram[i] -= lax.dot_general(
                weights, panel, (((0,), (0,)), ((), ())),
                precision=lax.Precision.HIGHEST, preferred_element_type=F32)
        return carry

    lax.fori_loop(0, RANK // PANEL, eliminate, 0)
    inverse = []
    for i in range(2):
        pivots = jnp.sum(jnp.where(row == col, gram[i, :, :RANK], 0.0), axis=1, keepdims=True)
        inverse.append(gram[i, :, RANK:] * lax.rsqrt(pivots))

    def solved(values, i):
        return lax.dot_general(
            values, inverse[i], (((1,), (1,)), ((), ())),
            precision=lax.Precision.HIGHEST, preferred_element_type=F32)

    left_u_out[...] = solved(raw_u[...], 0)
    left_d_out[...] = solved(raw_d[...], 1)

    def right_done(route, value):
        right_out[route] = solved(value, route) * (1.0 / (nz * ny))

    sent += scatter_rest(
        1, right_one, rpart_a, rpart_b, rgot_a, rgot_b, rsum_a, rsum_b, rfin_a, rfin_b, right_done)

    for copy in tok_sends:
        copy.wait_send()
    drain_first(warm_first + raw_first + sent)
    ring_drain(warm_ring)
    ring_drain(raw_ring)


def on_device(shape, activations, cotangent, gate_pre, up_value, hidden_grad, warm_factors):
    nz, ny, nt = shape
    tokens, width = activations.shape
    rows, ff = gate_pre.shape
    cut_b = 96 - CUT
    half = max(nz, ny) // 2
    out = pl.pallas_call(
        functools.partial(kernel, nz, ny, nt),
        out_shape=(
            jax.ShapeDtypeStruct((64, RANK), F32),
            jax.ShapeDtypeStruct((32, RANK), F32),
            jax.ShapeDtypeStruct((2, 64, RANK), F32)),
        in_specs=[pl.BlockSpec(memory_space=pl.ANY)] * 6,
        out_specs=[pl.BlockSpec(memory_space=pltpu.VMEM)] * 3,
        scratch_shapes=[
            pltpu.VMEM((nt, tokens, width), BF16),
            pltpu.VMEM((nt, tokens, width), BF16),
            pltpu.VMEM((rows, ff), BF16),
            pltpu.VMEM((rows, ff), BF16),
            pltpu.VMEM((rows, ff), BF16),
            pltpu.VMEM((2, nz, ny, 64, RANK), F32),
            pltpu.VMEM((rows, ff), BF16),
            pltpu.VMEM((rows, ff), BF16),
            pltpu.VMEM((rows, ff), BF16),
            pltpu.VMEM((nz, ny, CUT, RANK), BF16),
            pltpu.VMEM((nz, ny, cut_b, RANK), BF16),
            pltpu.VMEM((nz - 1, ny, CUT, RANK), BF16),
            pltpu.VMEM((ny - 1, nz, cut_b, RANK), BF16),
            pltpu.VMEM((ny, CUT, RANK), F32),
            pltpu.VMEM((nz, cut_b, RANK), F32),
            pltpu.VMEM((ny - 1, CUT, RANK), F32),
            pltpu.VMEM((nz - 1, cut_b, RANK), F32),
            pltpu.VMEM((64, RANK), F32),
            pltpu.VMEM((32, RANK), F32),
            pltpu.VMEM((nz, ny, 64, RANK), BF16),
            pltpu.VMEM((nz, ny, 32, RANK), BF16),
            pltpu.VMEM((nz, ny, 64, RANK), BF16),
            pltpu.VMEM((nz, ny, 64, RANK), BF16),
            pltpu.VMEM((nz - 1, ny, 64, RANK), BF16),
            pltpu.VMEM((ny - 1, nz, 64, RANK), BF16),
            pltpu.VMEM((ny, 64, RANK), F32),
            pltpu.VMEM((nz, 64, RANK), F32),
            pltpu.VMEM((ny - 1, 64, RANK), F32),
            pltpu.VMEM((nz - 1, 64, RANK), F32),
            pltpu.VMEM((2, RANK, 2 * RANK), F32),
            pltpu.SemaphoreType.DMA((7,)),
            pltpu.SemaphoreType.DMA((14,)),
            pltpu.SemaphoreType.DMA((14,)),
            pltpu.SemaphoreType.DMA((2, 3, max(nz, ny) - 1)),
            pltpu.SemaphoreType.DMA((2, 3, max(nz, ny) - 1)),
            pltpu.SemaphoreType.DMA((2, 4, half, 2, 2)),
            pltpu.SemaphoreType.DMA((2, 4, half, 2, 2)),
            pltpu.SemaphoreType.DMA((2, 2, max(nz, ny) - 1)),
            pltpu.SemaphoreType.DMA((2, 2, max(nz, ny) - 1)),
            pltpu.SemaphoreType.DMA((2, 2, max(nz, ny) - 1)),
            pltpu.SemaphoreType.DMA((2, 2, max(nz, ny) - 1)),
        ],
        compiler_params=pltpu.CompilerParams(
            collective_id=0, has_side_effects=True, vmem_limit_bytes=56 * 1024 * 1024),
        name="powersgd_step",
    )(activations, cotangent, gate_pre, up_value, hidden_grad, warm_factors)
    left_united, left_down, right = out
    return left_united[None], left_down[None], right[:, None]


def solution(mesh):
    dp, nt = mesh.shape["dp"], mesh.shape["tensor"]
    ny = 1 << (dp.bit_length() // 2)
    in_specs = (
        P(("dp", "tensor"), None),
        P(("dp", "tensor"), None),
        P("dp", "tensor"),
        P("dp", "tensor"),
        P("dp", "tensor"),
        P(None, "tensor", "dp", None),
    )
    out_specs = (P("tensor", "dp", None), P("tensor", "dp", None), P(None, "tensor", "dp", None))
    return jax.shard_map(
        functools.partial(on_device, (dp // ny, ny, nt)),
        mesh=mesh, in_specs=in_specs, out_specs=out_specs, check_vma=False)
```

time: 869 us -> 149 us (0.17)
  the two profiles are of different devices: /device:TPU:6 before, /device:TPU:22 now
where the time goes in v1:
time: 149 us
  Pallas kernels  145 us (97%)
  local copies, waits for them, and re-layouts  3.36 us (2%)
    pallas_call x1, Pallas kernels, on_device(): pl.pallas_call(functools.partial(kernel, nz, ny, nt), out_shape=(jax.Shap...  145 us
    unnamed x5, local copies, waits for them, and re-layouts  3.36 us

profile of v1, /device:TPU:22, one launch (start us, length us, event | category | flops | bytes accessed | tf_op | source)
XLA Modules:
  0.0 148.5 jit_solution(9558603852302298693)
XLA Ops:
  0.6 144.5 %powersgd_step.1 = (f32[64,128]{1,0:T(8,128)}, f32[32,128]{1,0:T(8,128)}, f32[2,64,128]{2,1,0:T(8,128)}) custom-call(bf16[32,4096]{1,0:T(8,128)(2,1)} %acts_in.1, bf16[32,4096]{1,0:T(8,128)(2,1)} %cot_in.1, bf16[256,2048]{1,0:T(8,128)(2,1)} %gate_in.1, bf16[256,2048]{1,0:T(8,128)(2,1)} %up_in.1, bf16[256,2048]{1,0:T(8,128)(2,1)} %hg_in.1, ...), custom_call_target="tpu_custom_call" | custom-call | tf_op jit(solution)/shard_map/powersgd_step/pallas_call | solution.py:428
  145.1 0.0 copy-start
  145.2 1.4 copy.13
  146.6 1.3 copy.14
  147.9 0.0 copy-done
  147.9 0.6 copy.15
Async XLA Ops:
  145.1 2.7 %copy-start = (f32[2,64,128]{2,1,0:T(8,128)S(1)}, f32[2,64,128]{2,1,0:T(8,128)}, u32[]{:S(2)}) copy-start(f32[2,64,128]{2,1,0:T(8,128)} %get-tuple-element.8) | copy-start | bytes 196612

commit v2 on v1

--- a/solution.py
+++ b/solution.py
@@ -11,6 +11,7 @@
 BF16 = jnp.bfloat16
 RANK = 128
 CUT = 48
+FINE = 32
 PANEL = 16
 
 
@@ -25,10 +26,10 @@
 
 
 def kernel(nz, ny, nt, acts_in, cot_in, gate_in, up_in, hg_in, warm_in,
-           left_u_out, left_d_out, right_out,
-           acts, cot, gate, up, hg, warm,
-           gate_back, up_back, hidden,
-           part_a, part_b, got_a, got_b, sum_a, sum_b, fin_a, fin_b,
+           packed_out,
+           acts, cot, gate, up, hg, warm_f, warm, fine,
+           united, hidden,
+           part_a, part_b, part_d, got_a, got_b, got_d, sum_a, sum_b, fin_a, fin_b,
            raw_u, raw_d, all_u, all_d,
            rpart_a, rpart_b, rgot_a, rgot_b, rsum_a, rsum_b, rfin_a, rfin_b,
            gram,
@@ -61,8 +62,7 @@
     loads = [
         pltpu.make_async_copy(src, dst, load_sem.at[i])
         for i, (src, dst) in enumerate([
-            (warm_in.at[0, 0], warm.at[0, z, y]), (warm_in.at[1, 0], warm.at[1, z, y]),
-            (gate_in, gate), (up_in, up), (hg_in, hg),
+            (warm_in, warm_f), (gate_in, gate), (up_in, up), (hg_in, hg),
             (acts_in, acts.at[t]), (cot_in, cot.at[t])])
     ]
     for load in loads:
@@ -82,8 +82,14 @@
         greet(at_z((z + k) % nz))
     for k in range(1, ny):
         greet(at_y((y + k) % ny))
-    for load in loads[:2]:
-        load.wait()
+    loads[0].wait()
+    coarse = 64 - FINE
+    fine[:, :, :, :coarse] = jnp.zeros((2, nz, ny, coarse, RANK), BF16)
+    for w in range(2):
+        values = warm_f[w, 0]
+        high = values.astype(BF16)
+        warm[w, z, y] = high
+        fine[w, z, y, coarse:] = (values - high.astype(F32)).astype(BF16)[coarse:]
     pl.semaphore_wait(barrier, 3 + nz - 1 + ny - 1)
 
     def exchange(n, me, place, src, dst, send, recv):
@@ -184,9 +190,15 @@
     def tok_wait(i, ref):
         remote(ref, ref, tok_send.at[i], tok_recv.at[i], to_twin).wait_recv()
 
+    def slow(w, zz, yy):
+        return fine.at[w, zz, yy, pl.ds(coarse, FINE)]
+
     warm_first = first_phase(0, [
         (True, lambda zz, yy: warm.at[0, zz, yy]), (False, lambda zz, yy: warm.at[1, zz, yy])])
+    fine_first = first_phase(2, [
+        (True, lambda zz, yy: slow(0, zz, yy)), (False, lambda zz, yy: slow(1, zz, yy))])
     start_first(warm_first)
+    start_first(fine_first)
     tok(0, acts_in, acts.at[here], to_right)
     tok(3, cot_in, cot.at[here], to_left)
     tok(1, cot_in, cot.at[here], to_right)
@@ -194,7 +206,7 @@
     tok(6, acts_in, acts.at[here], to_twin)
     tok(10, cot_in, cot.at[here], to_twin)
 
-    for load in loads[2:5]:
+    for load in loads[1:4]:
         load.wait()
 
     def backward(i, carry):
@@ -205,8 +217,8 @@
         sigma = jax.nn.sigmoid(gate_w)
         active = gate_w * sigma
         hidden[rows, :] = (active * up_w).astype(BF16)
-        gate_back[rows, :] = (hg_w * up_w * sigma * (1.0 + gate_w * (1.0 - sigma))).astype(BF16)
-        up_back[rows, :] = (hg_w * active).astype(BF16)
+        united[rows, :ff] = (hg_w * up_w * sigma * (1.0 + gate_w * (1.0 - sigma))).astype(BF16)
+        united[rows, ff:] = (hg_w * active).astype(BF16)
         return carry
 
     steps = gate_in.shape[0] // 16
@@ -218,7 +230,13 @@
         0,
         lambda b, h: [warm.at[0, b, pl.ds(h * halves_y, halves_y)]],
         lambda b, h: [warm.at[1, pl.ds(h * halves_z, halves_z), b]])
+    fine_ring = ring_streams(
+        2,
+        lambda b, h: [fine.at[0, b, pl.ds(h * halves_y, halves_y), pl.ds(coarse, FINE)]],
+        lambda b, h: [fine.at[1, pl.ds(h * halves_z, halves_z), b, pl.ds(coarse, FINE)]])
     ring_start(warm_ring)
+    wait_first(fine_first)
+    ring_start(fine_ring)
     lax.fori_loop(steps // 2, steps, backward, 0)
 
     tok_wait(0, acts.at[behind])
@@ -228,17 +246,19 @@
     tok(5, cot.at[ahead], cot.at[ahead], to_left)
     tok(12, cot.at[ahead], cot.at[ahead], to_twin)
     ring_advance(warm_ring, 0)
+    ring_advance(fine_ring, 0)
     tok_wait(2, acts.at[ahead])
     tok(8, acts.at[ahead], acts.at[ahead], to_twin)
     tok_wait(1, cot.at[behind])
     tok(11, cot.at[behind], cot.at[behind], to_twin)
     for step in range(1, max(nz, ny) // 2):
         ring_advance(warm_ring, step)
+        ring_advance(fine_ring, step)
     tok_wait(4, acts.at[across])
     tok(9, acts.at[across], acts.at[across], to_twin)
     tok_wait(5, cot.at[across])
     tok(13, cot.at[across], cot.at[across], to_twin)
-    for load in loads[5:]:
+    for load in loads[4:]:
         load.wait()
     for i in range(4):
         tok_wait(6 + i, acts.at[twin[i]])
@@ -248,62 +268,71 @@
         def body(i, total):
             columns = pl.ds(pl.multiple_of(i * tile, tile), tile)
             rows = tokens_ref[:, :, columns].reshape(nt * tokens, tile)
-            factor = two_halves(warm[w, i].reshape(tile, RANK))
+            factor = jnp.concatenate(
+                [warm[w, i].reshape(tile, RANK), fine[w, i].reshape(tile, RANK)], axis=1)
             return total + jnp.dot(rows, factor, preferred_element_type=F32)
 
         pair = lax.fori_loop(0, nz, body, jnp.zeros((nt * tokens, 2 * RANK), F32))
         return two_halves(pair[:, :RANK] + pair[:, RANK:])
 
-    probe_u = probe(acts, 0)
-    probe_d = probe(cot, 1)
-
     def folded(pair):
         return (pair[:, :RANK] + pair[:, RANK:]).astype(BF16)
 
-    per_tile = ff // tile
-
-    def raw_tile(source, first):
-        def body(i, carry):
-            columns = pl.ds(pl.multiple_of(i * tile, tile), tile)
-            block = folded(tdot(source[:, columns], probe_u)).reshape(ny, 64, RANK)
-            part_a[first + i] = block[:, :CUT]
-            part_b[first + i, :, :64 - CUT] = block[:, CUT:]
-            return carry
-        return body
-
-    lax.fori_loop(0, per_tile, raw_tile(gate_back, 0), 0)
-    lax.fori_loop(0, per_tile, raw_tile(up_back, per_tile), 0)
-
-    sends = []
-
-    def start_one(i, a, b, ga, gb):
-        plans = [
-            (nz, z, at_z, lambda to: a.at[to], lambda k, o: ga.at[k - 1], one_send.at[i, 0], one_recv.at[i, 0]),
-            (ny, y, at_y, lambda to: b.at[:, to], lambda k, o: gb.at[k - 1], one_send.at[i, 1], one_recv.at[i, 1])]
-        return plans
-
-    raw_one = start_one(0, part_a, part_b, got_a, got_b)
-    exchange(*raw_one[0])
+    def along_z(i, j, a, ga):
+        return (nz, z, at_z, lambda to: a.at[to], lambda k, o: ga.at[k - 1],
+                one_send.at[i, j], one_recv.at[i, j])
+
+    def along_y(i, j, b, gb):
+        return (ny, y, at_y, lambda to: b.at[:, to], lambda k, o: gb.at[k - 1],
+                one_send.at[i, j], one_recv.at[i, j])
+
+    def send_one(plan, k):
+        n, me, place, src, dst, send, recv = plan
+        to = (me + k) % n
+        remote(src(to), dst(k, me), send.at[k - 1], recv.at[k - 1], place(to)).start()
+
+    plan_a = along_z(0, 0, part_a, got_a)
+    plan_d = along_y(0, 1, part_d, got_d)
+    plan_b = along_y(0, 2, part_b, got_b)
+
+    probe_d = probe(cot, 1)
 
     def down_tile(i, carry):
         columns = pl.ds(pl.multiple_of(i * tile, tile), tile)
         block = folded(tdot(hidden[:, columns], probe_d)).reshape(2, ny, 32, RANK)
-        part_b[pl.ds(2 * i, 2), :, 64 - CUT:] = block
+        part_d[pl.ds(2 * i, 2)] = block
         return carry
 
-    lax.fori_loop(0, per_tile, down_tile, 0)
-    exchange(*raw_one[1])
-
-    def scatter_rest(i, plans, a, b, ga, gb, sa, sb, fa, fb, done):
-        sa[...] = a[z].astype(F32)
-        sb[...] = b[:, y].astype(F32)
+    lax.fori_loop(0, ff // tile, down_tile, 0)
+    exchange(*plan_d)
+
+    probe_u = probe(acts, 0)
+
+    def united_tile(k, carry):
+        i = (z + k) % nz
+        columns = pl.ds(pl.multiple_of(i * tile, tile), tile)
+        block = folded(tdot(united[:, columns], probe_u)).reshape(ny, 64, RANK)
+        part_a[i] = block[:, :CUT]
+        part_b[i] = block[:, CUT:]
+
+        @pl.when(k < nz)
+        def _():
+            send_one(plan_a, k)
+        return carry
+
+    lax.fori_loop(1, nz + 1, united_tile, 0)
+    exchange(*plan_b)
+
+    def scatter_rest(i, firsts_a, firsts_b, sa, sb, fa, fb, done):
         two = [
             (ny, y, at_y, lambda to: sa.at[to], lambda k, o: fa.at[k - 1], two_send.at[i, 0], two_recv.at[i, 0]),
             (nz, z, at_z, lambda to: sb.at[to], lambda k, o: fb.at[k - 1], two_send.at[i, 1], two_recv.at[i, 1])]
-        for plan, total, got, second in ((plans[0], sa, ga, two[0]), (plans[1], sb, gb, two[1])):
-            for k in range(1, plan[0]):
-                landed(*plan, k).wait_recv()
-                total[...] += got[k - 1].astype(F32)
+        for firsts, second in ((firsts_a, two[0]), (firsts_b, two[1])):
+            for plan, own, total, got in firsts:
+                total[...] = own[...].astype(F32)
+                for k in range(1, plan[0]):
+                    landed(*plan, k).wait_recv()
+                    total[...] += got[k - 1].astype(F32)
             exchange(*second)
         for route, (plan, total, fin, me) in enumerate(((two[0], sa, fa, y), (two[1], sb, fb, z))):
             value = total[me]
@@ -311,7 +340,7 @@
                 landed(*plan, k).wait_recv()
                 value = value + fin[k - 1]
             done(route, value)
-        return plans + two
+        return two
 
     def raw_done(route, value):
         if route == 0:
@@ -320,7 +349,11 @@
             raw_u[CUT:] = value[:64 - CUT]
             raw_d[...] = value[64 - CUT:]
 
-    sent = scatter_rest(0, raw_one, part_a, part_b, got_a, got_b, sum_a, sum_b, fin_a, fin_b, raw_done)
+    raw_two = scatter_rest(
+        0, [(plan_a, part_a.at[z], sum_a, got_a)],
+        [(plan_d, part_d.at[:, y], sum_b.at[:, pl.ds(64 - CUT, 32)], got_d),
+         (plan_b, part_b.at[:, y], sum_b.at[:, pl.ds(0, 64 - CUT)], got_b)],
+        sum_a, sum_b, fin_a, fin_b, raw_done)
 
     all_u[z, y] = raw_u[...].astype(BF16)
     all_d[z, y] = raw_d[...].astype(BF16)
@@ -341,25 +374,40 @@
         ring_advance(raw_ring, step)
 
     flat_u = all_u[...].reshape(2 * ff, RANK)
-    mixed_u = two_halves(
-        jnp.dot(gate_back[...], flat_u[:ff], preferred_element_type=F32)
-        + jnp.dot(up_back[...], flat_u[ff:], preferred_element_type=F32))
+    mixed_u = two_halves(jnp.dot(united[...], flat_u, preferred_element_type=F32))
     flat_d = all_d[...].reshape(ff, RANK)
     mixed_d = two_halves(jnp.dot(hidden[...], flat_d, preferred_element_type=F32))
-
-    def right_tile(source, mixed, target):
-        def body(i, carry):
+    rplan_a = along_z(1, 0, rpart_a, rgot_a)
+    rplan_b = along_y(1, 1, rpart_b, rgot_b)
+    rounds = ny // 2
+    per_round = nz // rounds
+
+    def right_round(q, carry):
+        for extra in range(per_round):
+            k = (q - 1) * per_round + extra + 1
+            i = (z + k) % nz
             columns = pl.ds(pl.multiple_of(i * tile, tile), tile)
-            rows = source[:, :, columns].reshape(nt * tokens, tile)
-            target[i] = folded(tdot(rows, mixed)).reshape(ny, 64, RANK)
-            return carry
-        return body
-
-    right_one = start_one(1, rpart_a, rpart_b, rgot_a, rgot_b)
-    lax.fori_loop(0, nz, right_tile(acts, mixed_u, rpart_a), 0)
-    exchange(*right_one[0])
-    lax.fori_loop(0, nz, right_tile(cot, mixed_d, rpart_b), 0)
-    exchange(*right_one[1])
+            rows = acts[:, :, columns].reshape(nt * tokens, tile)
+            rpart_a[i] = folded(tdot(rows, mixed_u)).reshape(ny, 64, RANK)
+
+            @pl.when(k < nz)
+            def _():
+                send_one(rplan_a, k)
+
+        pair = (y // 2 + q) % rounds
+        rows = jnp.concatenate(
+            [cot[:, :, pl.ds(pl.multiple_of(i * tile + pair * 128, 128), 128)].reshape(
+                nt * tokens, 128) for i in range(nz)], axis=1)
+        rpart_b[:, pl.ds(2 * pair, 2)] = folded(tdot(rows, mixed_d)).reshape(nz, 2, 64, RANK)
+        for extra in range(2):
+            to = 2 * pair + extra
+
+            @pl.when(to != y)
+            def _():
+                send_one(rplan_b, (to + ny - y) % ny)
+        return carry
+
+    lax.fori_loop(1, rounds + 1, right_round, 0)
 
     row = lax.broadcasted_iota(jnp.int32, (RANK, RANK), 0)
     col = lax.broadcasted_iota(jnp.int32, (RANK, RANK), 1)
@@ -403,20 +451,29 @@
             values, inverse[i], (((1,), (1,)), ((), ())),
             precision=lax.Precision.HIGHEST, preferred_element_type=F32)
 
-    left_u_out[...] = solved(raw_u[...], 0)
-    left_d_out[...] = solved(raw_d[...], 1)
-
-    def right_done(route, value):
-        right_out[route] = solved(value, route) * (1.0 / (nz * ny))
-
-    sent += scatter_rest(
-        1, right_one, rpart_a, rpart_b, rgot_a, rgot_b, rsum_a, rsum_b, rfin_a, rfin_b, right_done)
+    packed_out[:64] = solved(raw_u[...], 0)
+    packed_out[64:96] = solved(raw_d[...], 1)
 
     for copy in tok_sends:
         copy.wait_send()
-    drain_first(warm_first + raw_first + sent)
-    ring_drain(warm_ring)
-    ring_drain(raw_ring)
+    drain_first(warm_first + fine_first + raw_first + [plan_a, plan_d, plan_b] + raw_two)
+    for ring in (warm_ring, fine_ring, raw_ring):
+        ring_drain(ring)
+
+    def right_done(route, value):
+        packed_out[96 + 64 * route:160 + 64 * route] = solved(value, route) * (1.0 / (nz * ny))
+
+    right_two = scatter_rest(
+        1, [(rplan_a, rpart_a.at[z], rsum_a, rgot_a)], [(rplan_b, rpart_b.at[:, y], rsum_b, rgot_b)],
+        rsum_a, rsum_b, rfin_a, rfin_b, right_done)
+    drain_first([rplan_a, rplan_b] + right_two)
+
+
+def unpack(packed, left_u, left_d, right):
+    left_u[...] = packed[:64]
+    left_d[...] = packed[64:96]
+    right[0] = packed[96:160]
+    right[1] = packed[160:224]
 
 
 def on_device(shape, activations, cotangent, gate_pre, up_value, hidden_grad, warm_factors):
@@ -425,28 +482,28 @@
     rows, ff = gate_pre.shape
     cut_b = 96 - CUT
     half = max(nz, ny) // 2
-    out = pl.pallas_call(
+    packed = pl.pallas_call(
         functools.partial(kernel, nz, ny, nt),
-        out_shape=(
-            jax.ShapeDtypeStruct((64, RANK), F32),
-            jax.ShapeDtypeStruct((32, RANK), F32),
-            jax.ShapeDtypeStruct((2, 64, RANK), F32)),
+        out_shape=jax.ShapeDtypeStruct((224, RANK), F32),
         in_specs=[pl.BlockSpec(memory_space=pl.ANY)] * 6,
-        out_specs=[pl.BlockSpec(memory_space=pltpu.VMEM)] * 3,
+        out_specs=pl.BlockSpec(memory_space=pltpu.VMEM),
         scratch_shapes=[
             pltpu.VMEM((nt, tokens, width), BF16),
             pltpu.VMEM((nt, tokens, width), BF16),
             pltpu.VMEM((rows, ff), BF16),
             pltpu.VMEM((rows, ff), BF16),
             pltpu.VMEM((rows, ff), BF16),
-            pltpu.VMEM((2, nz, ny, 64, RANK), F32),
-            pltpu.VMEM((rows, ff), BF16),
-            pltpu.VMEM((rows, ff), BF16),
+            pltpu.VMEM((2, 1, 64, RANK), F32),
+            pltpu.VMEM((2, nz, ny, 64, RANK), BF16),
+            pltpu.VMEM((2, nz, ny, 64, RANK), BF16),
+            pltpu.VMEM((rows, 2 * ff), BF16),
             pltpu.VMEM((rows, ff), BF16),
             pltpu.VMEM((nz, ny, CUT, RANK), BF16),
-            pltpu.VMEM((nz, ny, cut_b, RANK), BF16),
+            pltpu.VMEM((nz, ny, 64 - CUT, RANK), BF16),
+            pltpu.VMEM((nz, ny, 32, RANK), BF16),
             pltpu.VMEM((nz - 1, ny, CUT, RANK), BF16),
-            pltpu.VMEM((ny - 1, nz, cut_b, RANK), BF16),
+            pltpu.VMEM((ny - 1, nz, 64 - CUT, RANK), BF16),
+            pltpu.VMEM((ny - 1, nz, 32, RANK), BF16),
             pltpu.VMEM((ny, CUT, RANK), F32),
             pltpu.VMEM((nz, cut_b, RANK), F32),
             pltpu.VMEM((ny - 1, CUT, RANK), F32),
@@ -464,15 +521,15 @@
             pltpu.VMEM((ny - 1, 64, RANK), F32),
             pltpu.VMEM((nz - 1, 64, RANK), F32),
             pltpu.VMEM((2, RANK, 2 * RANK), F32),
-            pltpu.SemaphoreType.DMA((7,)),
+            pltpu.SemaphoreType.DMA((6,)),
             pltpu.SemaphoreType.DMA((14,)),
             pltpu.SemaphoreType.DMA((14,)),
+            pltpu.SemaphoreType.DMA((3, 3, max(nz, ny) - 1)),
+            pltpu.SemaphoreType.DMA((3, 3, max(nz, ny) - 1)),
+            pltpu.SemaphoreType.DMA((3, 4, half, 2, 2)),
+            pltpu.SemaphoreType.DMA((3, 4, half, 2, 2)),
             pltpu.SemaphoreType.DMA((2, 3, max(nz, ny) - 1)),
             pltpu.SemaphoreType.DMA((2, 3, max(nz, ny) - 1)),
-            pltpu.SemaphoreType.DMA((2, 4, half, 2, 2)),
-            pltpu.SemaphoreType.DMA((2, 4, half, 2, 2)),
-            pltpu.SemaphoreType.DMA((2, 2, max(nz, ny) - 1)),
-            pltpu.SemaphoreType.DMA((2, 2, max(nz, ny) - 1)),
             pltpu.SemaphoreType.DMA((2, 2, max(nz, ny) - 1)),
             pltpu.SemaphoreType.DMA((2, 2, max(nz, ny) - 1)),
         ],
@@ -480,7 +537,14 @@
             collective_id=0, has_side_effects=True, vmem_limit_bytes=56 * 1024 * 1024),
         name="powersgd_step",
     )(activations, cotangent, gate_pre, up_value, hidden_grad, warm_factors)
-    left_united, left_down, right = out
+    left_united, left_down, right = pl.pallas_call(
+        unpack,
+        out_shape=(
+            jax.ShapeDtypeStruct((64, RANK), F32),
+            jax.ShapeDtypeStruct((32, RANK), F32),
+            jax.ShapeDtypeStruct((2, 64, RANK), F32)),
+        name="unpack",
+    )(packed)
     return left_united[None], left_down[None], right[:, None]
 
 

time: 149 us -> 136 us (0.913)
  the two profiles are of different devices: /device:TPU:22 before, /device:TPU:6 now
where the time goes in v2:
time: 136 us; the launch traced here: 134 us
  Pallas kernels  133 us (98%)
    pallas_call x1, Pallas kernels, on_device(): pl.pallas_call(functools.partial(kernel, nz, ny, nt), out_shape=jax.Shape...  132 us

profile of v2, /device:TPU:6, one launch (start us, length us, event | category | flops | bytes accessed | tf_op | source)
XLA Modules:
  0.0 133.8 jit_solution(11091983889257648313)
XLA Ops:
  0.6 131.6 %powersgd_step.1.packed = f32[224,128]{1,0:T(8,128)} custom-call(bf16[32,4096]{1,0:T(8,128)(2,1)} %acts_in.1, bf16[32,4096]{1,0:T(8,128)(2,1)} %cot_in.1, bf16[256,2048]{1,0:T(8,128)(2,1)} %gate_in.1, bf16[256,2048]{1,0:T(8,128)(2,1)} %up_in.1, bf16[256,2048]{1,0:T(8,128)(2,1)} %hg_in.1, f32[2,1,64,128]{3,2,1,0:T(8,128)} %warm_in.1), custom_call_target="tpu_custom_call" | custom-call | tf_op jit(solution)/shard_map/powersgd_step/pallas_call | solution.py:485
  132.2 1.5 %unpack.1 = (f32[64,128]{1,0:T(8,128)}, f32[32,128]{1,0:T(8,128)}, f32[2,64,128]{2,1,0:T(8,128)}) custom-call(f32[224,128]{1,0:T(8,128)} %powersgd_step.1.packed), custom_call_target="tpu_custom_call" | custom-call | tf_op jit(solution)/shard_map/unpack/pallas_call | solution.py:540

commit v3 on v2

--- a/solution.py
+++ b/solution.py
@@ -27,14 +27,14 @@
 
 def kernel(nz, ny, nt, acts_in, cot_in, gate_in, up_in, hg_in, warm_in,
            packed_out,
-           acts, cot, gate, up, hg, warm_f, warm, fine,
+           acts, cot, gate, up, hg, warm_f, warm,
            united, hidden,
            part_a, part_b, part_d, got_a, got_b, got_d, sum_a, sum_b, fin_a, fin_b,
-           raw_u, raw_d, all_u, all_d,
+           raw_u, raw_d, everyone,
            rpart_a, rpart_b, rgot_a, rgot_b, rsum_a, rsum_b, rfin_a, rfin_b,
-           gram,
+           gram, relay_a, relay_d, relay_b, rrelay_a, rrelay_b, keep_a, rkeep_a,
            load_sem, tok_send, tok_recv, first_send, first_recv,
-           ring_send, ring_recv, one_send, one_recv, two_send, two_recv):
+           ring_send, ring_recv, one_send, one_recv, two_send, two_recv, relay_send, relay_recv):
     d = lax.axis_index("dp")
     t = lax.axis_index("tensor")
     z, y = d // ny, d % ny
@@ -84,12 +84,11 @@
         greet(at_y((y + k) % ny))
     loads[0].wait()
     coarse = 64 - FINE
-    fine[:, :, :, :coarse] = jnp.zeros((2, nz, ny, coarse, RANK), BF16)
     for w in range(2):
         values = warm_f[w, 0]
         high = values.astype(BF16)
-        warm[w, z, y] = high
-        fine[w, z, y, coarse:] = (values - high.astype(F32)).astype(BF16)[coarse:]
+        warm[w, z, y, :64] = high
+        warm[w, z, y, 64:] = (values - high.astype(F32)).astype(BF16)[coarse:]
     pl.semaphore_wait(barrier, 3 + nz - 1 + ny - 1)
 
     def exchange(n, me, place, src, dst, send, recv):
@@ -125,18 +124,16 @@
             for k in range(1, plan[0]):
                 landed(*plan, k).wait_send()
 
-    def ring_copies(streams, step, half, i, receiving):
+    def ring_copy(streams, step, half, i, receiving):
         n, me, place, pieces, turn, which = streams[i]
         if receiving:
             block = (me + n - turn * (1 + step)) % n
         else:
             block = (me + n - turn * step) % n
         to = (me + n + turn) % n
-        return [
-            remote(ref, ref, ring_send.at[which, i, step, half, j],
-                   ring_recv.at[which, i, step, half, j], place(to))
-            for j, ref in enumerate(pieces(block, half))
-        ]
+        ref = pieces(block, half)
+        return remote(ref, ref, ring_send.at[which, i, step, half],
+                      ring_recv.at[which, i, step, half], place(to))
 
     def ring_moves(n, turn, step):
         if step < n // 2 - 1:
@@ -148,8 +145,7 @@
             for i, (n, _, _, _, turn, _) in enumerate(streams):
                 halves = ring_moves(n, turn, 0)
                 if order < len(halves):
-                    for copy in ring_copies(streams, 0, halves[order], i, False):
-                        copy.start()
+                    ring_copy(streams, 0, halves[order], i, False).start()
 
     def ring_advance(streams, step):
         for order in range(2):
@@ -159,18 +155,15 @@
                 halves = ring_moves(n, turn, step)
                 if order < len(halves):
                     half = halves[order]
-                    for copy in ring_copies(streams, step, half, i, True):
-                        copy.wait_recv()
+                    ring_copy(streams, step, half, i, True).wait_recv()
                     if step + 1 < n // 2 and half in ring_moves(n, turn, step + 1):
-                        for copy in ring_copies(streams, step + 1, half, i, False):
-                            copy.start()
+                        ring_copy(streams, step + 1, half, i, False).start()
 
     def ring_drain(streams):
         for i, (n, _, _, _, turn, _) in enumerate(streams):
             for step in range(n // 2):
                 for half in ring_moves(n, turn, step):
-                    for copy in ring_copies(streams, step, half, i, False):
-                        copy.wait_send()
+                    ring_copy(streams, step, half, i, False).wait_send()
 
     def ring_streams(which, z_pieces, y_pieces):
         return [
@@ -190,15 +183,9 @@
     def tok_wait(i, ref):
         remote(ref, ref, tok_send.at[i], tok_recv.at[i], to_twin).wait_recv()
 
-    def slow(w, zz, yy):
-        return fine.at[w, zz, yy, pl.ds(coarse, FINE)]
-
     warm_first = first_phase(0, [
         (True, lambda zz, yy: warm.at[0, zz, yy]), (False, lambda zz, yy: warm.at[1, zz, yy])])
-    fine_first = first_phase(2, [
-        (True, lambda zz, yy: slow(0, zz, yy)), (False, lambda zz, yy: slow(1, zz, yy))])
     start_first(warm_first)
-    start_first(fine_first)
     tok(0, acts_in, acts.at[here], to_right)
     tok(3, cot_in, cot.at[here], to_left)
     tok(1, cot_in, cot.at[here], to_right)
@@ -228,15 +215,9 @@
     halves_y, halves_z = ny // 2, nz // 2
     warm_ring = ring_streams(
         0,
-        lambda b, h: [warm.at[0, b, pl.ds(h * halves_y, halves_y)]],
-        lambda b, h: [warm.at[1, pl.ds(h * halves_z, halves_z), b]])
-    fine_ring = ring_streams(
-        2,
-        lambda b, h: [fine.at[0, b, pl.ds(h * halves_y, halves_y), pl.ds(coarse, FINE)]],
-        lambda b, h: [fine.at[1, pl.ds(h * halves_z, halves_z), b, pl.ds(coarse, FINE)]])
+        lambda b, h: warm.at[0, b, pl.ds(h * halves_y, halves_y)],
+        lambda b, h: warm.at[1, pl.ds(h * halves_z, halves_z), b])
     ring_start(warm_ring)
-    wait_first(fine_first)
-    ring_start(fine_ring)
     lax.fori_loop(steps // 2, steps, backward, 0)
 
     tok_wait(0, acts.at[behind])
@@ -246,14 +227,12 @@
     tok(5, cot.at[ahead], cot.at[ahead], to_left)
     tok(12, cot.at[ahead], cot.at[ahead], to_twin)
     ring_advance(warm_ring, 0)
-    ring_advance(fine_ring, 0)
     tok_wait(2, acts.at[ahead])
     tok(8, acts.at[ahead], acts.at[ahead], to_twin)
     tok_wait(1, cot.at[behind])
     tok(11, cot.at[behind], cot.at[behind], to_twin)
     for step in range(1, max(nz, ny) // 2):
         ring_advance(warm_ring, step)
-        ring_advance(fine_ring, step)
     tok_wait(4, acts.at[across])
     tok(9, acts.at[across], acts.at[across], to_twin)
     tok_wait(5, cot.at[across])
@@ -264,19 +243,22 @@
         tok_wait(6 + i, acts.at[twin[i]])
         tok_wait(10 + i, cot.at[twin[i]])
 
+    no_fine = jnp.zeros((ny, coarse, RANK), BF16)
+
     def probe(tokens_ref, w):
         def body(i, total):
             columns = pl.ds(pl.multiple_of(i * tile, tile), tile)
             rows = tokens_ref[:, :, columns].reshape(nt * tokens, tile)
             factor = jnp.concatenate(
-                [warm[w, i].reshape(tile, RANK), fine[w, i].reshape(tile, RANK)], axis=1)
+                [warm[w, i, :, :64].reshape(tile, RANK),
+                 jnp.concatenate([no_fine, warm[w, i, :, 64:]], axis=1).reshape(tile, RANK)], axis=1)
             return total + jnp.dot(rows, factor, preferred_element_type=F32)
 
         pair = lax.fori_loop(0, nz, body, jnp.zeros((nt * tokens, 2 * RANK), F32))
         return two_halves(pair[:, :RANK] + pair[:, RANK:])
 
     def folded(pair):
-        return (pair[:, :RANK] + pair[:, RANK:]).astype(BF16)
+        return pair[:, :RANK] + pair[:, RANK:]
 
     def along_z(i, j, a, ga):
         return (nz, z, at_z, lambda to: a.at[to], lambda k, o: ga.at[k - 1],
@@ -291,6 +273,53 @@
         to = (me + k) % n
         remote(src(to), dst(k, me), send.at[k - 1], recv.at[k - 1], place(to)).start()
 
+    def near(n):
+        return [k for k in range(1, n) if abs(k - n // 2) > 1]
+
+    def arriving(n):
+        return [k for k in range(1, n) if k != n // 2]
+
+    def is_near(k, n):
+        return (k != 0) & (k != n // 2) & (k != n // 2 - 1) & (k != n // 2 + 1)
+
+    def in_order(j, n):
+        j = (j + n - 1) % n
+        m, odd = (j + 1) // 2, j % 2
+        return (odd * m + (1 - odd) * (n - m)) % n
+
+    def relay_copies(plan, r, relay):
+        n, me, place, src = plan[:4]
+        block = src((me + n // 2) % n)
+        size = relay.shape[1]
+        return [
+            remote(block.at[pl.ds(h * size, size)], relay.at[h], relay_send.at[r, h],
+                   relay_recv.at[r, h], place((me + (1, n - 1)[h]) % n)) for h in range(2)]
+
+    def far_out(plan, r, relay):
+        for copy in relay_copies(plan, r, relay):
+            copy.start()
+
+    def near_out(plan):
+        for k in near(plan[0]):
+            send_one(plan, k)
+
+    def relayed(plan, r, relay, keep):
+        n, me, place, src = plan[:4]
+        size = relay.shape[1]
+        for h, copy in enumerate(relay_copies(plan, r, relay)):
+            copy.wait_recv()
+            k = n // 2 - 1 + 2 * h
+            piece = src((me + k) % n).at[pl.ds(h * size, size)]
+            own = piece if keep is None else keep.at[h, pl.ds(h * size, size)]
+            piece[...] = (own[...].astype(F32) + relay[h].astype(F32)).astype(BF16)
+            send_one(plan, k)
+
+    def drain_one(plan, r, relay):
+        for copy in relay_copies(plan, r, relay):
+            copy.wait_send()
+        for k in arriving(plan[0]):
+            landed(*plan, k).wait_send()
+
     plan_a = along_z(0, 0, part_a, got_a)
     plan_d = along_y(0, 1, part_d, got_d)
     plan_b = along_y(0, 2, part_b, got_b)
@@ -300,28 +329,54 @@
     def down_tile(i, carry):
         columns = pl.ds(pl.multiple_of(i * tile, tile), tile)
         block = folded(tdot(hidden[:, columns], probe_d)).reshape(2, ny, 32, RANK)
-        part_d[pl.ds(2 * i, 2)] = block
+        part_d[pl.ds(2 * i, 2)] = block.astype(BF16)
         return carry
 
     lax.fori_loop(0, ff // tile, down_tile, 0)
-    exchange(*plan_d)
+    far_out(plan_d, 1, relay_d)
+    near_out(plan_d)
 
     probe_u = probe(acts, 0)
 
-    def united_tile(k, carry):
+    def row_out(j, plan, r, relay, keep, total, store, compute):
+        k = in_order(j, nz)
         i = (z + k) % nz
-        columns = pl.ds(pl.multiple_of(i * tile, tile), tile)
-        block = folded(tdot(united[:, columns], probe_u)).reshape(ny, 64, RANK)
+        block = folded(compute(pl.ds(pl.multiple_of(i * tile, tile), tile))).reshape(ny, 64, RANK)
+        store(i, block.astype(BF16))
+        rows = total.shape[1]
+
+        @pl.when(k == 0)
+        def _():
+            total[...] = block[:, :rows]
+
+        for h in range(2):
+            @pl.when(k == nz // 2 - 1 + 2 * h)
+            def _():
+                keep[h] = block[:, :rows]
+
+        @pl.when(k == nz // 2)
+        def _():
+            far_out(plan, r, relay)
+
+        @pl.when(is_near(k, nz))
+        def _():
+            send_one(plan, k)
+
+    def store_raw(i, block):
         part_a[i] = block[:, :CUT]
         part_b[i] = block[:, CUT:]
 
-        @pl.when(k < nz)
-        def _():
-            send_one(plan_a, k)
+    def united_tile(j, carry):
+        row_out(j, plan_a, 0, relay_a, keep_a, sum_a, store_raw,
+                lambda columns: tdot(united[:, columns], probe_u))
         return carry
 
-    lax.fori_loop(1, nz + 1, united_tile, 0)
-    exchange(*plan_b)
+    lax.fori_loop(0, nz, united_tile, 0)
+    far_out(plan_b, 2, relay_b)
+    relayed(plan_a, 0, relay_a, keep_a)
+    near_out(plan_b)
+    relayed(plan_d, 1, relay_d, None)
+    relayed(plan_b, 2, relay_b, None)
 
     def scatter_rest(i, firsts_a, firsts_b, sa, sb, fa, fb, done):
         two = [
@@ -329,8 +384,9 @@
             (nz, z, at_z, lambda to: sb.at[to], lambda k, o: fb.at[k - 1], two_send.at[i, 1], two_recv.at[i, 1])]
         for firsts, second in ((firsts_a, two[0]), (firsts_b, two[1])):
             for plan, own, total, got in firsts:
-                total[...] = own[...].astype(F32)
-                for k in range(1, plan[0]):
+                if own is not None:
+                    total[...] = own[...].astype(F32)
+                for k in arriving(plan[0]):
                     landed(*plan, k).wait_recv()
                     total[...] += got[k - 1].astype(F32)
             exchange(*second)
@@ -350,64 +406,64 @@
             raw_d[...] = value[64 - CUT:]
 
     raw_two = scatter_rest(
-        0, [(plan_a, part_a.at[z], sum_a, got_a)],
+        0, [(plan_a, None, sum_a, got_a)],
         [(plan_d, part_d.at[:, y], sum_b.at[:, pl.ds(64 - CUT, 32)], got_d),
          (plan_b, part_b.at[:, y], sum_b.at[:, pl.ds(0, 64 - CUT)], got_b)],
         sum_a, sum_b, fin_a, fin_b, raw_done)
 
-    all_u[z, y] = raw_u[...].astype(BF16)
-    all_d[z, y] = raw_d[...].astype(BF16)
+    everyone[z, y, :64] = raw_u[...].astype(BF16)
+    everyone[z, y, 64:] = raw_d[...].astype(BF16)
     raw_first = first_phase(1, [
-        (True, lambda zz, yy: all_u.at[zz, yy, pl.ds(0, CUT)]),
-        (False, lambda zz, yy: all_u.at[zz, yy, pl.ds(CUT, 64 - CUT)]),
-        (False, lambda zz, yy: all_d.at[zz, yy])])
+        (True, lambda zz, yy: everyone.at[zz, yy, pl.ds(0, CUT)]),
+        (False, lambda zz, yy: everyone.at[zz, yy, pl.ds(CUT, 96 - CUT)])])
     start_first(raw_first)
     raw_ring = ring_streams(
         1,
-        lambda b, h: [all_u.at[b, pl.ds(h * halves_y, halves_y), pl.ds(0, CUT)]],
-        lambda b, h: [
-            all_u.at[pl.ds(h * halves_z, halves_z), b, pl.ds(CUT, 64 - CUT)],
-            all_d.at[pl.ds(h * halves_z, halves_z), b]])
+        lambda b, h: everyone.at[b, pl.ds(h * halves_y, halves_y), pl.ds(0, CUT)],
+        lambda b, h: everyone.at[pl.ds(h * halves_z, halves_z), b, pl.ds(CUT, 96 - CUT)])
     wait_first(raw_first)
     ring_start(raw_ring)
     for step in range(max(nz, ny) // 2):
         ring_advance(raw_ring, step)
 
-    flat_u = all_u[...].reshape(2 * ff, RANK)
+    flat_u = everyone[:, :, :64].reshape(2 * ff, RANK)
     mixed_u = two_halves(jnp.dot(united[...], flat_u, preferred_element_type=F32))
-    flat_d = all_d[...].reshape(ff, RANK)
+    flat_d = everyone[:, :, 64:].reshape(ff, RANK)
     mixed_d = two_halves(jnp.dot(hidden[...], flat_d, preferred_element_type=F32))
     rplan_a = along_z(1, 0, rpart_a, rgot_a)
     rplan_b = along_y(1, 1, rpart_b, rgot_b)
     rounds = ny // 2
     per_round = nz // rounds
 
+    def store_right(i, block):
+        rpart_a[i] = block
+
     def right_round(q, carry):
         for extra in range(per_round):
-            k = (q - 1) * per_round + extra + 1
-            i = (z + k) % nz
-            columns = pl.ds(pl.multiple_of(i * tile, tile), tile)
-            rows = acts[:, :, columns].reshape(nt * tokens, tile)
-            rpart_a[i] = folded(tdot(rows, mixed_u)).reshape(ny, 64, RANK)
-
-            @pl.when(k < nz)
-            def _():
-                send_one(rplan_a, k)
-
-        pair = (y // 2 + q) % rounds
+            row_out(q * per_round + extra, rplan_a, 3, rrelay_a, rkeep_a, rsum_a, store_right,
+                    lambda columns: tdot(acts[:, :, columns].reshape(nt * tokens, tile), mixed_u))
+
+        pair = (y // 2 + q + rounds // 2) % rounds
         rows = jnp.concatenate(
             [cot[:, :, pl.ds(pl.multiple_of(i * tile + pair * 128, 128), 128)].reshape(
                 nt * tokens, 128) for i in range(nz)], axis=1)
-        rpart_b[:, pl.ds(2 * pair, 2)] = folded(tdot(rows, mixed_d)).reshape(nz, 2, 64, RANK)
+        rpart_b[:, pl.ds(2 * pair, 2)] = folded(
+            tdot(rows, mixed_d)).reshape(nz, 2, 64, RANK).astype(BF16)
         for extra in range(2):
-            to = 2 * pair + extra
-
-            @pl.when(to != y)
+            k = (2 * pair + extra + ny - y) % ny
+
+            @pl.when(k == ny // 2)
             def _():
-                send_one(rplan_b, (to + ny - y) % ny)
+                far_out(rplan_b, 4, rrelay_b)
+
+            @pl.when(is_near(k, ny))
+            def _():
+                send_one(rplan_b, k)
         return carry
 
-    lax.fori_loop(1, rounds + 1, right_round, 0)
+    lax.fori_loop(0, rounds, right_round, 0)
+    relayed(rplan_a, 3, rrelay_a, rkeep_a)
+    relayed(rplan_b, 4, rrelay_b, None)
 
     row = lax.broadcasted_iota(jnp.int32, (RANK, RANK), 0)
     col = lax.broadcasted_iota(jnp.int32, (RANK, RANK), 1)
@@ -456,17 +512,22 @@
 
     for copy in tok_sends:
         copy.wait_send()
-    drain_first(warm_first + fine_first + raw_first + [plan_a, plan_d, plan_b] + raw_two)
-    for ring in (warm_ring, fine_ring, raw_ring):
+    drain_first(warm_first + raw_first + raw_two)
+    drain_one(plan_a, 0, relay_a)
+    drain_one(plan_d, 1, relay_d)
+    drain_one(plan_b, 2, relay_b)
+    for ring in (warm_ring, raw_ring):
         ring_drain(ring)
 
     def right_done(route, value):
         packed_out[96 + 64 * route:160 + 64 * route] = solved(value, route) * (1.0 / (nz * ny))
 
     right_two = scatter_rest(
-        1, [(rplan_a, rpart_a.at[z], rsum_a, rgot_a)], [(rplan_b, rpart_b.at[:, y], rsum_b, rgot_b)],
+        1, [(rplan_a, None, rsum_a, rgot_a)], [(rplan_b, rpart_b.at[:, y], rsum_b, rgot_b)],
         rsum_a, rsum_b, rfin_a, rfin_b, right_done)
-    drain_first([rplan_a, rplan_b] + right_two)
+    drain_first(right_two)
+    drain_one(rplan_a, 3, rrelay_a)
+    drain_one(rplan_b, 4, rrelay_b)
 
 
 def unpack(packed, left_u, left_d, right):
@@ -494,8 +555,7 @@
             pltpu.VMEM((rows, ff), BF16),
             pltpu.VMEM((rows, ff), BF16),
             pltpu.VMEM((2, 1, 64, RANK), F32),
-            pltpu.VMEM((2, nz, ny, 64, RANK), BF16),
-            pltpu.VMEM((2, nz, ny, 64, RANK), BF16),
+            pltpu.VMEM((2, nz, ny, 64 + FINE, RANK), BF16),
             pltpu.VMEM((rows, 2 * ff), BF16),
             pltpu.VMEM((rows, ff), BF16),
             pltpu.VMEM((nz, ny, CUT, RANK), BF16),
@@ -510,8 +570,7 @@
             pltpu.VMEM((nz - 1, cut_b, RANK), F32),
             pltpu.VMEM((64, RANK), F32),
             pltpu.VMEM((32, RANK), F32),
-            pltpu.VMEM((nz, ny, 64, RANK), BF16),
-            pltpu.VMEM((nz, ny, 32, RANK), BF16),
+            pltpu.VMEM((nz, ny, 96, RANK), BF16),
             pltpu.VMEM((nz, ny, 64, RANK), BF16),
             pltpu.VMEM((nz, ny, 64, RANK), BF16),
             pltpu.VMEM((nz - 1, ny, 64, RANK), BF16),
@@ -521,17 +580,26 @@
             pltpu.VMEM((ny - 1, 64, RANK), F32),
             pltpu.VMEM((nz - 1, 64, RANK), F32),
             pltpu.VMEM((2, RANK, 2 * RANK), F32),
+            pltpu.VMEM((2, ny // 2, CUT, RANK), BF16),
+            pltpu.VMEM((2, nz // 2, 32, RANK), BF16),
+            pltpu.VMEM((2, nz // 2, 64 - CUT, RANK), BF16),
+            pltpu.VMEM((2, ny // 2, 64, RANK), BF16),
+            pltpu.VMEM((2, nz // 2, 64, RANK), BF16),
+            pltpu.VMEM((2, ny, CUT, RANK), F32),
+            pltpu.VMEM((2, ny, 64, RANK), F32),
             pltpu.SemaphoreType.DMA((6,)),
             pltpu.SemaphoreType.DMA((14,)),
             pltpu.SemaphoreType.DMA((14,)),
-            pltpu.SemaphoreType.DMA((3, 3, max(nz, ny) - 1)),
-            pltpu.SemaphoreType.DMA((3, 3, max(nz, ny) - 1)),
-            pltpu.SemaphoreType.DMA((3, 4, half, 2, 2)),
-            pltpu.SemaphoreType.DMA((3, 4, half, 2, 2)),
+            pltpu.SemaphoreType.DMA((2, 2, max(nz, ny) - 1)),
+            pltpu.SemaphoreType.DMA((2, 2, max(nz, ny) - 1)),
+            pltpu.SemaphoreType.DMA((2, 4, half, 2)),
+            pltpu.SemaphoreType.DMA((2, 4, half, 2)),
             pltpu.SemaphoreType.DMA((2, 3, max(nz, ny) - 1)),
             pltpu.SemaphoreType.DMA((2, 3, max(nz, ny) - 1)),
             pltpu.SemaphoreType.DMA((2, 2, max(nz, ny) - 1)),
             pltpu.SemaphoreType.DMA((2, 2, max(nz, ny) - 1)),
+            pltpu.SemaphoreType.DMA((5, 2)),
+            pltpu.SemaphoreType.DMA((5, 2)),
         ],
         compiler_params=pltpu.CompilerParams(
             collective_id=0, has_side_effects=True, vmem_limit_bytes=56 * 1024 * 1024),

time: 136 us -> 130 us (0.956)
  Pallas kernels: 133 us -> 128 us
    pallas_call x1, Pallas kernels: 132 us -> 126 us  [on_device(): pl.pallas_call(functools.partial(kernel, nz, ny, nt), out_shape=jax.Shape...]
where the time goes in v3:
time: 130 us; the launch traced here: 129 us
  Pallas kernels  128 us (98%)
    pallas_call x1, Pallas kernels, on_device(): pl.pallas_call(functools.partial(kernel, nz, ny, nt), out_shape=jax.Shape...  126 us

profile of v3, /device:TPU:6, one launch (start us, length us, event | category | flops | bytes accessed | tf_op | source)
XLA Modules:
  0.0 128.7 jit_solution(18315517798690571300)
XLA Ops:
  0.6 126.5 %powersgd_step.1.packed = f32[224,128]{1,0:T(8,128)} custom-call(bf16[32,4096]{1,0:T(8,128)(2,1)} %acts_in.1, bf16[32,4096]{1,0:T(8,128)(2,1)} %cot_in.1, bf16[256,2048]{1,0:T(8,128)(2,1)} %gate_in.1, bf16[256,2048]{1,0:T(8,128)(2,1)} %up_in.1, bf16[256,2048]{1,0:T(8,128)(2,1)} %hg_in.1, f32[2,1,64,128]{3,2,1,0:T(8,128)} %warm_in.1), custom_call_target="tpu_custom_call" | custom-call | tf_op jit(solution)/shard_map/powersgd_step/pallas_call | solution.py:546
  127.1 1.5 %unpack.1 = (f32[64,128]{1,0:T(8,128)}, f32[32,128]{1,0:T(8,128)}, f32[2,64,128]{2,1,0:T(8,128)}) custom-call(f32[224,128]{1,0:T(8,128)} %powersgd_step.1.packed), custom_call_target="tpu_custom_call" | custom-call | tf_op jit(solution)/shard_map/unpack/pallas_call | solution.py:608

commit v4 on v3

--- a/solution.py
+++ b/solution.py
@@ -34,7 +34,7 @@
            rpart_a, rpart_b, rgot_a, rgot_b, rsum_a, rsum_b, rfin_a, rfin_b,
            gram, relay_a, relay_d, relay_b, rrelay_a, rrelay_b, keep_a, rkeep_a,
            load_sem, tok_send, tok_recv, first_send, first_recv,
-           ring_send, ring_recv, one_send, one_recv, two_send, two_recv, relay_send, relay_recv):
+           ring_send, ring_recv, one_send, one_recv, two_send, two_recv, relay_send, relay_recv, hop_send, hop_recv):
     d = lax.axis_index("dp")
     t = lax.axis_index("tensor")
     z, y = d // ny, d % ny
@@ -140,9 +140,10 @@
             return (0, 1) if turn > 0 else (1, 0)
         return (0,) if turn > 0 else (1,)
 
-    def ring_start(streams):
+    def ring_start(streams, route):
         for order in range(2):
-            for i, (n, _, _, _, turn, _) in enumerate(streams):
+            for i in (2 * route, 2 * route + 1):
+                n, turn = streams[i][0], streams[i][4]
                 halves = ring_moves(n, turn, 0)
                 if order < len(halves):
                     ring_copy(streams, 0, halves[order], i, False).start()
@@ -211,13 +212,14 @@
     steps = gate_in.shape[0] // 16
     lax.fori_loop(0, steps // 2, backward, 0)
 
-    wait_first(warm_first)
     halves_y, halves_z = ny // 2, nz // 2
     warm_ring = ring_streams(
         0,
         lambda b, h: warm.at[0, b, pl.ds(h * halves_y, halves_y)],
         lambda b, h: warm.at[1, pl.ds(h * halves_z, halves_z), b])
-    ring_start(warm_ring)
+    for route in range(2):
+        wait_first(warm_first[route:route + 1])
+        ring_start(warm_ring, route)
     lax.fori_loop(steps // 2, steps, backward, 0)
 
     tok_wait(0, acts.at[behind])
@@ -243,18 +245,19 @@
         tok_wait(6 + i, acts.at[twin[i]])
         tok_wait(10 + i, cot.at[twin[i]])
 
-    no_fine = jnp.zeros((ny, coarse, RANK), BF16)
+    group = nz // 2
+    no_fine = jnp.zeros((group, ny, coarse, RANK), BF16)
 
     def probe(tokens_ref, w):
-        def body(i, total):
-            columns = pl.ds(pl.multiple_of(i * tile, tile), tile)
-            rows = tokens_ref[:, :, columns].reshape(nt * tokens, tile)
+        pair = jnp.zeros((nt * tokens, 2 * RANK), F32)
+        for i in range(nz // group):
+            span = group * tile
+            rows = tokens_ref[:, :, i * span:(i + 1) * span].reshape(nt * tokens, span)
+            blocks = warm[w, i * group:(i + 1) * group]
             factor = jnp.concatenate(
-                [warm[w, i, :, :64].reshape(tile, RANK),
-                 jnp.concatenate([no_fine, warm[w, i, :, 64:]], axis=1).reshape(tile, RANK)], axis=1)
-            return total + jnp.dot(rows, factor, preferred_element_type=F32)
-
-        pair = lax.fori_loop(0, nz, body, jnp.zeros((nt * tokens, 2 * RANK), F32))
+                [blocks[:, :, :64].reshape(span, RANK),
+                 jnp.concatenate([no_fine, blocks[:, :, 64:]], axis=2).reshape(span, RANK)], axis=1)
+            pair = pair + jnp.dot(rows, factor, preferred_element_type=F32)
         return two_halves(pair[:, :RANK] + pair[:, RANK:])
 
     def folded(pair):
@@ -398,12 +401,19 @@
             done(route, value)
         return two
 
+    raw_first = first_phase(1, [
+        (True, lambda zz, yy: everyone.at[zz, yy, pl.ds(0, CUT)]),
+        (False, lambda zz, yy: everyone.at[zz, yy, pl.ds(CUT, 96 - CUT)])])
+
     def raw_done(route, value):
         if route == 0:
             raw_u[:CUT] = value
+            everyone[z, y, :CUT] = value.astype(BF16)
         else:
             raw_u[CUT:] = value[:64 - CUT]
             raw_d[...] = value[64 - CUT:]
+            everyone[z, y, CUT:] = value.astype(BF16)
+        start_first(raw_first[route:route + 1])
 
     raw_two = scatter_rest(
         0, [(plan_a, None, sum_a, got_a)],
@@ -411,20 +421,40 @@
          (plan_b, part_b.at[:, y], sum_b.at[:, pl.ds(0, 64 - CUT)], got_b)],
         sum_a, sum_b, fin_a, fin_b, raw_done)
 
-    everyone[z, y, :64] = raw_u[...].astype(BF16)
-    everyone[z, y, 64:] = raw_d[...].astype(BF16)
-    raw_first = first_phase(1, [
-        (True, lambda zz, yy: everyone.at[zz, yy, pl.ds(0, CUT)]),
-        (False, lambda zz, yy: everyone.at[zz, yy, pl.ds(CUT, 96 - CUT)])])
-    start_first(raw_first)
-    raw_ring = ring_streams(
-        1,
-        lambda b, h: everyone.at[b, pl.ds(h * halves_y, halves_y), pl.ds(0, CUT)],
-        lambda b, h: everyone.at[pl.ds(h * halves_z, halves_z), b, pl.ds(CUT, 96 - CUT)])
-    wait_first(raw_first)
-    ring_start(raw_ring)
-    for step in range(max(nz, ny) // 2):
-        ring_advance(raw_ring, step)
+    def hops(route):
+        n, me, place = ((nz, z, at_z), (ny, y, at_y))[route]
+
+        def block(offset, half=None):
+            b = (me + n + offset) % n
+            if route == 0:
+                part = slice(None) if half is None else pl.ds(half * halves_y, halves_y)
+                return everyone.at[b, part, pl.ds(0, CUT)]
+            part = slice(None) if half is None else pl.ds(half * halves_z, halves_z)
+            return everyone.at[part, b, pl.ds(CUT, 96 - CUT)]
+
+        def copy(i, ref, offset):
+            return remote(ref, ref, hop_send.at[route, i], hop_recv.at[route, i],
+                          place((me + n + offset) % n))
+
+        sent = [copy(0, block(0), 2), copy(1, block(0), -2), copy(2, block(0), 1), copy(3, block(0), -1),
+                copy(4, block(-2), 1), copy(5, block(2), -1), copy(6, block(-2, 0), 2), copy(7, block(2, 1), -2)]
+        came = [copy(0, block(-2), 2), copy(1, block(2), -2), copy(2, block(-1), 1), copy(3, block(1), -1),
+                copy(4, block(-3), 1), copy(5, block(3), -1), copy(6, block(-4, 0), 2), copy(7, block(4, 1), -2)]
+        return sent, came
+
+    raw_hops = [hops(0), hops(1)]
+    for route in range(2):
+        wait_first(raw_first[route:route + 1])
+        for copy in raw_hops[route][0][:4]:
+            copy.start()
+    for side in range(2):
+        for sent, came in raw_hops:
+            came[side].wait_recv()
+            sent[4 + side].start()
+            sent[6 + side].start()
+    for sent, came in raw_hops:
+        for copy in came[2:]:
+            copy.wait_recv()
 
     flat_u = everyone[:, :, :64].reshape(2 * ff, RANK)
     mixed_u = two_halves(jnp.dot(united[...], flat_u, preferred_element_type=F32))
@@ -516,8 +546,10 @@
     drain_one(plan_a, 0, relay_a)
     drain_one(plan_d, 1, relay_d)
     drain_one(plan_b, 2, relay_b)
-    for ring in (warm_ring, raw_ring):
-        ring_drain(ring)
+    ring_drain(warm_ring)
+    for sent, came in raw_hops:
+        for copy in sent:
+            copy.wait_send()
 
     def right_done(route, value):
         packed_out[96 + 64 * route:160 + 64 * route] = solved(value, route) * (1.0 / (nz * ny))
@@ -600,6 +632,8 @@
             pltpu.SemaphoreType.DMA((2, 2, max(nz, ny) - 1)),
             pltpu.SemaphoreType.DMA((5, 2)),
             pltpu.SemaphoreType.DMA((5, 2)),
+            pltpu.SemaphoreType.DMA((2, 8)),
+            pltpu.SemaphoreType.DMA((2, 8)),
         ],
         compiler_params=pltpu.CompilerParams(
             collective_id=0, has_side_effects=True, vmem_limit_bytes=56 * 1024 * 1024),

time: 130 us -> 125 us (0.962)
  Pallas kernels: 128 us -> 123 us
    pallas_call x1, Pallas kernels: 126 us -> 121 us  [on_device(): pl.pallas_call(functools.partial(kernel, nz, ny, nt), out_shape=jax.Shape...]
where the time goes in v4:
time: 125 us; the launch traced here: 124 us
  Pallas kernels  123 us (98%)
    pallas_call x1, Pallas kernels, on_device(): pl.pallas_call(functools.partial(kernel, nz, ny, nt), out_shape=jax.Shape...  121 us

profile of v4, /device:TPU:6, one launch (start us, length us, event | category | flops | bytes accessed | tf_op | source)
XLA Modules:
  0.0 123.5 jit_solution(14638310896100297856)
XLA Ops:
  0.6 121.4 %powersgd_step.1.packed = f32[224,128]{1,0:T(8,128)} custom-call(bf16[32,4096]{1,0:T(8,128)(2,1)} %acts_in.1, bf16[32,4096]{1,0:T(8,128)(2,1)} %cot_in.1, bf16[256,2048]{1,0:T(8,128)(2,1)} %gate_in.1, bf16[256,2048]{1,0:T(8,128)(2,1)} %up_in.1, bf16[256,2048]{1,0:T(8,128)(2,1)} %hg_in.1, f32[2,1,64,128]{3,2,1,0:T(8,128)} %warm_in.1), custom_call_target="tpu_custom_call" | custom-call | tf_op jit(solution)/shard_map/powersgd_step/pallas_call | solution.py:578
  122.0 1.5 %unpack.1 = (f32[64,128]{1,0:T(8,128)}, f32[32,128]{1,0:T(8,128)}, f32[2,64,128]{2,1,0:T(8,128)}) custom-call(f32[224,128]{1,0:T(8,128)} %powersgd_step.1.packed), custom_call_target="tpu_custom_call" | custom-call | tf_op jit(solution)/shard_map/unpack/pallas_call | solution.py:642

commit v5 on v4

--- a/solution.py
+++ b/solution.py
@@ -233,16 +233,16 @@
     tok(8, acts.at[ahead], acts.at[ahead], to_twin)
     tok_wait(1, cot.at[behind])
     tok(11, cot.at[behind], cot.at[behind], to_twin)
-    for step in range(1, max(nz, ny) // 2):
-        ring_advance(warm_ring, step)
+    ring_advance(warm_ring, 1)
     tok_wait(4, acts.at[across])
     tok(9, acts.at[across], acts.at[across], to_twin)
     tok_wait(5, cot.at[across])
     tok(13, cot.at[across], cot.at[across], to_twin)
+    for step in range(2, max(nz, ny) // 2):
+        ring_advance(warm_ring, step)
     for load in loads[4:]:
         load.wait()
     for i in range(4):
-        tok_wait(6 + i, acts.at[twin[i]])
         tok_wait(10 + i, cot.at[twin[i]])
 
     group = nz // 2
@@ -329,16 +329,14 @@
 
     probe_d = probe(cot, 1)
 
-    def down_tile(i, carry):
-        columns = pl.ds(pl.multiple_of(i * tile, tile), tile)
-        block = folded(tdot(hidden[:, columns], probe_d)).reshape(2, ny, 32, RANK)
-        part_d[pl.ds(2 * i, 2)] = block.astype(BF16)
-        return carry
-
-    lax.fori_loop(0, ff // tile, down_tile, 0)
+    for i in range(2):
+        block = folded(tdot(hidden[:, i * ff // 2:(i + 1) * ff // 2], probe_d))
+        part_d[i * nz // 2:(i + 1) * nz // 2] = block.reshape(nz // 2, ny, 32, RANK).astype(BF16)
     far_out(plan_d, 1, relay_d)
     near_out(plan_d)
 
+    for i in range(4):
+        tok_wait(6 + i, acts.at[twin[i]])
     probe_u = probe(acts, 0)
 
     def row_out(j, plan, r, relay, keep, total, store, compute):

time: 125 us -> 123 us (0.984)
  Pallas kernels: 123 us -> 121 us
    pallas_call x1, Pallas kernels: 121 us -> 120 us  [on_device(): pl.pallas_call(functools.partial(kernel, nz, ny, nt), out_shape=jax.Shape...]
where the time goes in v5:
time: 123 us; the launch traced here: 122 us
  Pallas kernels  121 us (98%)
    pallas_call x1, Pallas kernels, on_device(): pl.pallas_call(functools.partial(kernel, nz, ny, nt), out_shape=jax.Shape...  120 us

profile of v5, /device:TPU:6, one launch (start us, length us, event | category | flops | bytes accessed | tf_op | source)
XLA Modules:
  0.0 122.0 jit_solution(14859666318286278491)
XLA Ops:
  0.6 119.8 %powersgd_step.1.packed = f32[224,128]{1,0:T(8,128)} custom-call(bf16[32,4096]{1,0:T(8,128)(2,1)} %acts_in.1, bf16[32,4096]{1,0:T(8,128)(2,1)} %cot_in.1, bf16[256,2048]{1,0:T(8,128)(2,1)} %gate_in.1, bf16[256,2048]{1,0:T(8,128)(2,1)} %up_in.1, bf16[256,2048]{1,0:T(8,128)(2,1)} %hg_in.1, f32[2,1,64,128]{3,2,1,0:T(8,128)} %warm_in.1), custom_call_target="tpu_custom_call" | custom-call | tf_op jit(solution)/shard_map/powersgd_step/pallas_call | solution.py:576
  120.4 1.5 %unpack.1 = (f32[64,128]{1,0:T(8,128)}, f32[32,128]{1,0:T(8,128)}, f32[2,64,128]{2,1,0:T(8,128)}) custom-call(f32[224,128]{1,0:T(8,128)} %powersgd_step.1.packed), custom_call_target="tpu_custom_call" | custom-call | tf_op jit(solution)/shard_map/unpack/pallas_call | solution.py:640
